TPU v7x, 32 devices: a whole 2x2x4 slice. The times are simulated.
32 devices in a mesh: parts: 2 (over x), blk: 16 (over z, y, core).
Axes of the slice: x: 2, y: 2, z: 4, core: 2. Of those that a mesh axis runs over, the one named last changes fastest.
Arguments:
- right_side: float32 [5, 8192, 128], P(None, ('parts', 'blk')), parts along dimension 1, may hold values from -24 to 24
- off_diag: bfloat16 [4, 5, 5, 8192, 128], P(None, None, None, ('parts', 'blk')), parts along dimension 3, may hold values from -3 to 3
- diag_block: float32 [5, 5, 8192, 128], P(None, None, ('parts', 'blk')), parts along dimension 2, may hold values from -1.2 to 12, as said below
- block_of_device: int32 [16], replicated, may hold values from 0 to 4, as said below
- interface_pairs: int32 [16, 2], P('blk'), may hold values from -1 to 28, as said below
- strip_order: int32 [16, 2, 128], P('blk'), may hold values from 0 to 127, as said below
Outputs:
- update: float32 [5, 8192, 128], P(None, ('parts', 'blk')), parts along dimension 1
There are 2 independent parts, one for each index of `parts`. A program takes and returns all parts, laid end to end along the dimension named above; an argument that names none is the same for every part. Nothing has to cross between parts.
Inputs may be any that keep to these rules, and one draw needn't show every extreme that they name: `block_of_device`: each of the 5 blocks is a nonempty run of consecutive devices on the cycle of devices; block 0 begins at device 16 - 2 and holds devices 16 - 2, 15 and 0, and the block numbers rise by one at each block start after device 0. `interface_pairs`: at the first device of a block (column 0) and at its last device (column 1) the entry is 2 p + t, naming the matched end: device p, its first-row side (t = 0) or last-row side (t = 1), which is itself the first or last device of a block. The matching pairs up all 10 block ends and is mutual. All other entries are -1. `strip_order`: each row is either 0, 1, ..., 127 or its reversal; the two sides of a matched pair use the same one; sides that are no block end hold 0, 1, ..., 127. `diag_block`: in every cell's 5x5 block, each diagonal entry exceeds the sum of the magnitudes of the other entries of its row.
All inputs are finite; a program needn't handle non-finite values.
Results may differ from a plain program's by a relative error of at most 0.0003.
Values sent between devices are 32-bit elements; how exact they have to be, the bound alone decides.
No kernel may reach another device: no remote copies, remote signals or barrier semaphores. Data moves between devices by JAX's collectives and lax.ppermute only.
A program may use at most 128 MiB of HBM per device.

v0:
```python
import jax
import jax.numpy as jnp
from jax import lax
from jax.sharding import PartitionSpec as P

SWEEPS = 2


def shifted(value, axis, by):
    count = lax.axis_size(axis)
    return lax.ppermute(value, axis, [(i, (i + by) % count) for i in range(count)])


def factor(diag_block):
    entries = [[diag_block[row_at, col_at] for col_at in range(5)] for row_at in range(5)]
    multipliers = {}
    for pivot_at in range(5):
        for row_at in range(pivot_at + 1, 5):
            scale_now = entries[row_at][pivot_at] / entries[pivot_at][pivot_at]
            multipliers[row_at, pivot_at] = scale_now
            for col_at in range(pivot_at + 1, 5):
                entries[row_at][col_at] = (
                    entries[row_at][col_at] - scale_now * entries[pivot_at][col_at]
                )
    return (multipliers, entries)


def substitute(factors, vector):
    multipliers, upper_rows = factors
    forward = []
    for row_at in range(5):
        running = vector[row_at]
        for col_at in range(row_at):
            running = running - multipliers[row_at, col_at] * forward[col_at]
        forward.append(running)
    result = [None] * 5
    for row_at in reversed(range(5)):
        running = forward[row_at]
        for col_at in range(row_at + 1, 5):
            running = running - upper_rows[row_at][col_at] * result[col_at]
        result[row_at] = running / upper_rows[row_at][row_at]
    return jnp.stack(result)


def couple(off_diag, neighbours):
    coupled = jnp.zeros(neighbours[0].shape, jnp.float32)
    for face in range(4):
        for component in range(5):
            coupled = coupled + off_diag[face, :, component] * neighbours[face][component][None]
    return coupled


def on_device(right_side, off_diag, diag_block, block_of_device, interface_pairs, strip_order):
    axis_size = lax.axis_size("blk")
    my_index = lax.axis_index("blk")
    rows_here = right_side.shape[1]
    factors = factor(diag_block)
    update = substitute(factors, [right_side[component] for component in range(5)])
    own_block = block_of_device[my_index]
    prev_block = block_of_device[(my_index + axis_size - 1) % axis_size]
    next_block = block_of_device[(my_index + 1) % axis_size]
    first_end = prev_block != own_block
    last_end = next_block != own_block
    end_codes = jnp.maximum(interface_pairs[0], 0)
    partner = end_codes // 2
    partner_side = end_codes % 2
    orders = strip_order[0]
    zero_column = jnp.zeros((5, rows_here, 1), jnp.float32)
    for sweep_no in range(SWEEPS):
        edge_pair = jnp.stack([update[:, 0], update[:, -1]])
        from_below = shifted(edge_pair[1], "blk", 1)
        from_above = shifted(edge_pair[0], "blk", -1)
        everything = lax.all_gather(edge_pair[None], "blk", axis=0, tiled=True)
        incoming = everything[partner, partner_side]
        strips = jnp.take_along_axis(incoming, orders[:, None, :], axis=2)
        west_edge = jnp.where(first_end, strips[0], from_below)
        east_edge = jnp.where(last_end, strips[1], from_above)
        west_side = jnp.concatenate([west_edge[:, None], update[:, :-1]], axis=1)
        east_side = jnp.concatenate([update[:, 1:], east_edge[:, None]], axis=1)
        south_side = jnp.concatenate([zero_column, update[:, :, :-1]], axis=2)
        north_side = jnp.concatenate([update[:, :, 1:], zero_column], axis=2)
        coupled = couple(off_diag, [west_side, east_side, south_side, north_side])
        update = substitute(
            factors, [right_side[component] - coupled[component] for component in range(5)]
        )
    return update


def solution(mesh):
    return jax.shard_map(
        on_device,
        mesh=mesh,
        in_specs=(
            P(None, ("parts", "blk"), None),
            P(None, None, None, ("parts", "blk"), None),
            P(None, None, ("parts", "blk"), None),
            P(),
            P("blk", None),
            P("blk", None, None),
        ),
        out_specs=P(None, ("parts", "blk"), None),
        check_vma=False,
    )
```

profile of v0, /device:TPU:0, one launch (start us, length us, event | category | flops | bytes accessed | tf_op | source)
XLA Modules:
  0.0 143.5 jit_solution(5321616445039784245)
XLA Ops:
  0.0 1.1 bitcast_divide_fusion.1
  1.1 1.3 fusion.104
  2.3 1.9 %fusion.103 = (f32[1,1,256,128]{3,2,1,0:T(8,128)S(1)}, f32[1,1,256,128]{3,2,1,0:T(8,128)S(1)}, f32[1,1,256,128]{3,2,1,0:T(8,128)S(1)}, f32[1,1,256,128]{3,2,1,0:...) fusion(f32[5,5,256,128]{3,2,1,0:T(8,128)} %param.10), kind=kLoop, calls=%fused_computation.293 | loop fusion | bytes 4980736 | tf_op jit(solution)/shard_map/slice | solution.py:15
  4.3 0.6 copy-done.28
  5.0 0.2 multiply_subtract_fusion.11
  5.2 0.0 copy-done.30
  5.3 0.0 copy-start.97
  5.3 1.4 subtract_divide_fusion.7
  6.7 0.0 copy-done.65
  6.7 0.0 copy-done.62
  6.8 1.1 stack.10
  7.9 0.6 slice_bitcast_fusion.4
  8.5 0.5 collective-permute-start
  8.9 5.0 %collective-permute-start.1 = (f32[5,128]{1,0:T(8,128)}, f32[5,128]{1,0:T(8,128)}, u32[]{:S(2)}, u32[]{:S(2)}) collective-permute-start(f32[5,128]{1,0:T(8,128)} %get-tuple-element.99), channel_id=1, source_target_pairs={{0,15},{1,0},{2,1},{3,2},{4,3},{5,4},{6,5},{7,6},{8,7},{9,8},{10,9... | collective-permute-start | bytes 7688 | tf_op jit(solution)/shard_map/ppermute | solution.py:11
  13.9 0.0 copy-done.97
  13.9 0.5 and_bitcast_fusion
  14.5 1.4 %fusion.105 = (f32[5,255,128]{2,0,1:T(8,128)}, f32[5,255,128]{2,0,1:T(8,128)}) fusion(f32[5,256,128]{2,0,1:T(8,128)S(1)} %stack.10), kind=kLoop, calls=%fused_computation.295 | loop fusion | bytes 2611200 | tf_op jit(solution)/shard_map/slice | solution.py:78
  15.9 0.3 fusion.106
  16.3 19.7 %all-gather = f32[32,5,128]{2,1,0:T(8,128)S(1)} all-gather(f32[2,5,128]{2,1,0:T(8,128)S(1)} %pad_maximum_fusion.12), channel_id=2, replica_groups=mesh['parts'=2,'blk'=16] {'blk'}, dimensions={0}, use_global_device_ids=true | all-gather | bytes 87040 | tf_op jit(solution)/shard_map/all_gather | solution.py:73
  36.0 0.6 gather_fusion
  36.6 0.1 copy.196
  36.7 1.9 %gather_fusion.2 = f32[256,5]{1,0:T(8,128)S(1)} fusion(f32[2,5,128]{1,2,0:T(8,128)S(1)} %copy.196, s32[256]{0:T(256)S(1)} %fusion.91), kind=kCustom, calls=%fused_computation.clone | custom fusion | bytes 12288 | tf_op jit(solution)/shard_map/jit(take_along_axis)/gather | solution.py:75
  38.6 0.7 copy.198
  39.3 5.5 %fusion.102 = (bf16[1,5,1,256,128]{4,3,2,1,0:T(8,128)(2,1)}, bf16[1,5,1,256,128]{4,3,2,1,0:T(8,128)(2,1)}, bf16[1,5,1,256,128]{4,3,2,1,0:T(8,128)(2,1)}, bf16[1,...) fusion(bf16[4,5,5,256,128]{4,3,2,1,0:T(8,128)(2,1)} %param.9), kind=kLoop, calls=%fused_computation.292 | loop fusion | bytes 12451840 | tf_op jit(solution)/shard_map/slice | solution.py:49
  44.8 2.8 %pad_slice_fusion.12 = (f32[1,256,128]{2,0,1:T(1,128)}, f32[1,256,128]{2,0,1:T(1,128)}, f32[1,256,128]{2,0,1:T(1,128)}, f32[1,256,128]{2,0,1:T(1,128)}, f32[1,25...) fusion(f32[5,256,127]{2,0,1:T(8,128)S(1)} %get-tuple-element.11, ...), kind=kLoop, calls=%fused_computation.94 | loop fusion | bytes 2611200 | tf_op jit(solution)/shard_map/slice | solution.py:49
  47.7 1.9 %slice.454 = bf16[1,5,1,256,128]{4,3,2,1,0:T(8,128)(2,1)} slice(bf16[4,5,5,256,128]{4,3,2,1,0:T(8,128)(2,1)} %param.9), slice={[3:4], [0:5], [4:5], [0:256], [0:128]} | slice | bytes 655360 | tf_op jit(solution)/shard_map/slice | solution.py:49
  49.6 0.0 copy-start.15
  49.7 1.5 %fusion.111 = (s32[1]{0:T(128)}, s32[1]{0:T(128)}, s32[1]{0:T(128)}) fusion(s32[16]{0:T(128)} %param.11, s32[]{:T(128)S(6)} %select_n.96, s32[]{:T(128)S(6)} %select_n.105, s32[]{:T(128)S(6)} %select_n.97), kind=kLoop, calls=%fused_computation.301 | loop fusion | bytes 36 | tf_op jit(solution)/shard_map/dynamic_slice | solution.py:60
  53.7 0.0 collective-permute-done
  53.7 0.0 collective-permute-done.1
  53.7 0.7 fusion.89
  54.4 4.0 %pad_maximum_fusion.11 = (f32[1,256,128]{2,0,1:T(1,128)S(1)}, f32[1,256,128]{2,0,1:T(1,128)S(1)}, f32[1,256,128]{2,0,1:T(1,128)S(1)}, f32[1,256,128]{2,0,1:T(1,128)S(1)}, f32[1,256,128]{2,0,1:T(1,128)S(1)}) fusion(f32[5,255,128]{2,0,1:T(8,128)} %get-tuple-element.102, f32[5,1,128]{2,0,1:T(8,128)S(1)} %get-tuple-element.155), kind=kLoop, calls=%fused_computation.200 | loop fusion | flops 163840 | bytes 1310720 | tf_op jit(solution)/shard_map/slice | solution.py:49
  58.4 0.5 pad_maximum_fusion.6
  59.3 17.9 %fusion.18 = f32[5,256,128]{2,0,1:T(8,128)S(1)} fusion(bf16[1,5,1,256,128]{4,3,2,1,0:T(8,128)(2,1)} %slice.454, bf16[1,5,1,256,128]{4,3,2,1,0:T(8,128)(2,1)S(1)} %copy-done.2, bf16[1,5,1,256,128]{4,3,2,1,0:T(8,128)(2,1)S(1)} %copy-done.3, bf16[1,5,1,256,128]{4,3,2,1,0:T(8,128)(2,1)S(1)} %copy-done.4, bf16[1,5,1,256,128]{4,3,2,1,0:T(8,128)(2,1)S(1)} %copy-done.5, ...), kind=kLoop, calls=%fused_computation.70 | loop fusion | flops 9666560 | bytes 9830400 | tf_op jit(solution)/shard_map/add | solution.py:49
  77.3 0.9 multiply_subtract_fusion.5
  78.3 1.5 %multiply_subtract_fusion.4 = (f32[1,256,128]{2,0,1:T(1,128)S(1)}, f32[1,256,128]{2,0,1:T(1,128)S(1)}, f32[1,256,128]{2,0,1:T(1,128)S(1)}, f32[1,256,128]{2,0,1:T(1,128)S(1)}, f32[1,256,128]{2,0,1:T(1,128)S(1)}) fusion(f32[1,256,128]{2,0,1:T(1,128)S(1)} %bitcast.528, f32[1,256,128]{2,0,1:T(1,128)S(1)} %bitcast.503, f32[1,256,128]{2,0,1:T(1,128)S(1)} %bitcast.466, ...), kind=kLoop, calls=%fused_computation.215 | loop fusion | flops 1081344 | bytes 3801088 | tf_op jit(solution)/shard_map/sub | solution.py:40
  79.8 0.9 fusion.82
  80.9 1.1 fusion.107
  82.0 1.3 fusion.109
  83.3 0.1 collective-permute-start.3
  83.4 0.5 collective-permute-start.2
  83.9 20.4 %all-gather.1 = f32[32,5,128]{2,1,0:T(8,128)} all-gather(f32[2,5,128]{2,1,0:T(8,128)S(1)} %pad_maximum_fusion.13), channel_id=3, replica_groups=mesh['parts'=2,'blk'=16] {'blk'}, dimensions={0}, use_global_device_ids=true | all-gather | bytes 87040 | tf_op jit(solution)/shard_map/all_gather | solution.py:73
  104.3 1.5 %gather_fusion.1 = f32[2,5,128]{2,1,0:T(8,128)S(1)} fusion(f32[16,2,5,128]{3,2,1,0:T(8,128)} %bitcast.586, s32[2]{0:T(128)S(1)} %fusion.97), kind=kCustom, calls=%fused_computation.3 | custom fusion | bytes 10256 | tf_op jit(solution)/shard_map/gather | solution.py:74
  105.7 0.8 copy.226
  106.5 2.6 %gather_fusion.3 = f32[256,5]{1,0:T(8,128)} fusion(f32[2,5,128]{1,2,0:T(8,128)} %copy.226, s32[256]{0:T(256)S(1)} %fusion.91), kind=kCustom, calls=%fused_computation.1.clone | custom fusion | bytes 12288 | tf_op jit(solution)/shard_map/jit(take_along_axis)/gather | solution.py:75
  109.1 1.0 copy.228
  110.1 0.0 copy-start.16
  110.2 1.5 %fusion.38 = (f32[256,128]{1,0:T(8,128)S(1)}, f32[256,128]{1,0:T(8,128)S(1)}, f32[256,128]{1,0:T(8,128)S(1)}, f32[256,128]{1,0:T(8,128)S(1)}, f32[256,128]{1,0:T(8,128)S(1)}) fusion(f32[5,256,127]{2,1,0:T(8,128)} %get-tuple-element.140), kind=kLoop, calls=%fused_computation.138 | loop fusion | bytes 1305600 | tf_op jit(solution)/shard_map/mul | solution.py:49
  111.7 1.2 fusion.43
  113.0 0.0 collective-permute-done.3
  113.0 0.0 collective-permute-done.2
  113.0 1.2 fusion.59
  114.2 1.2 fusion.51
  115.7 22.0 %fusion.37 = f32[5,256,128]{2,0,1:T(8,128)S(1)} fusion(bf16[1,5,1,256,128]{4,3,2,1,0:T(8,128)(2,1)S(1)} %copy-done.27, bf16[1,5,1,256,128]{4,3,2,1,0:T(8,128)(2,1)S(1)} %copy-done.2, bf16[1,5,1,256,128]{4,3,2,1,0:T(8,128)(2,1)S(1)} %copy-done.3, bf16[1,5,1,256,128]{4,3,2,1,0:T(8,128)(2,1)S(1)} %copy-done.4, bf16[1,5,1,256,128]{4,3,2,1,0:T(8,128)(2,1)S(1)} %copy-done.5, ...), kind=kLoop, calls=%fused_computation.89 | loop fusion | flops 9666560 | bytes 9830400 | tf_op jit(solution)/shard_map/add | solution.py:49
  137.9 0.3 slice_subtract_fusion.4
  138.2 1.1 multiply_subtract_fusion.3
  139.4 1.0 multiply_subtract_fusion.1
  140.5 0.1 fusion.98
  140.6 0.1 mul.1981
  140.8 0.1 multiply_subtract_fusion
  140.9 1.0 fusion.81
  142.0 0.0 copy-start.94
  142.0 0.8 copy-done.94
  142.8 0.7 constant_dynamic-update-slice_fusion.4
  (210 shorter events, 0.7 us)
Async XLA Ops:
  5.3 8.6 %copy-start.97 = (s32[1,2,128]{2,1,0:T(2,128)S(1)}, s32[1,2,128]{2,1,0:T(2,128)}, u32[]{:S(2)}) copy-start(s32[1,2,128]{2,1,0:T(2,128)} %param.13) | copy-start | bytes 3076
  8.5 45.2 %collective-permute-start = (f32[5,128]{1,0:T(8,128)}, f32[5,128]{1,0:T(8,128)}, u32[]{:S(2)}, u32[]{:S(2)}) collective-permute-start(f32[5,128]{1,0:T(8,128)} %get-tuple-element.98), channel_id=1, source_target_pairs={{0,1},{1,2},{2,3},{3,4},{4,5},{5,6},{6,7},{7,8},{8,9},{9,10},{10,1... | collective-permute-start | bytes 7688 | tf_op jit(solution)/shard_map/ppermute | solution.py:11
  8.9 44.8 %collective-permute-start.1 = (f32[5,128]{1,0:T(8,128)}, f32[5,128]{1,0:T(8,128)}, u32[]{:S(2)}, u32[]{:S(2)}) collective-permute-start(f32[5,128]{1,0:T(8,128)} %get-tuple-element.99), channel_id=1, source_target_pairs={{0,15},{1,0},{2,1},{3,2},{4,3},{5,4},{6,5},{7,6},{8,7},{9,8},{10,9... | collective-permute-start | bytes 7688 | tf_op jit(solution)/shard_map/ppermute | solution.py:11
  39.3 5.5 %copy-start.93 = (f32[2,128,5]{1,2,0:T(8,128)S(1)}, f32[2,128,5]{1,2,0:T(8,128)}, u32[]{:S(2)}) copy-start(f32[2,128,5]{1,2,0:T(8,128)} %copy.198) | copy-start | bytes 15364
  39.3 5.5 %copy-start.95 = (pred[2,128]{1,0:T(4,128)(4,1)S(1)}, pred[2,128]{1,0:T(4,128)(4,1)}, u32[]{:S(2)}) copy-start(pred[2,128]{1,0:T(4,128)(4,1)} %and_bitcast_fusion) | copy-start | bytes 772
  44.8 13.6 %copy-start = (f32[5,255,128]{2,0,1:T(8,128)S(1)}, f32[5,255,128]{2,0,1:T(8,128)}, u32[]{:S(2)}) copy-start(f32[5,255,128]{2,0,1:T(8,128)} %get-tuple-element.103) | copy-start | bytes 1958404
  47.7 11.2 %copy-start.1 = (bf16[1,5,1,256,128]{4,3,2,1,0:T(8,128)(2,1)S(1)}, bf16[1,5,1,256,128]{4,3,2,1,0:T(8,128)(2,1)}, u32[]{:S(2)}) copy-start(bf16[1,5,1,256,128]{4,3,2,1,0:T(8,128)(2,1)} %get-tuple-element.48) | copy-start | bytes 983044
  47.7 11.2 %copy-start.2 = (bf16[1,5,1,256,128]{4,3,2,1,0:T(8,128)(2,1)S(1)}, bf16[1,5,1,256,128]{4,3,2,1,0:T(8,128)(2,1)}, u32[]{:S(2)}) copy-start(bf16[1,5,1,256,128]{4,3,2,1,0:T(8,128)(2,1)} %get-tuple-element.49) | copy-start | bytes 983044
  47.7 11.2 %copy-start.3 = (bf16[1,5,1,256,128]{4,3,2,1,0:T(8,128)(2,1)S(1)}, bf16[1,5,1,256,128]{4,3,2,1,0:T(8,128)(2,1)}, u32[]{:S(2)}) copy-start(bf16[1,5,1,256,128]{4,3,2,1,0:T(8,128)(2,1)} %get-tuple-element.50) | copy-start | bytes 983044
  47.7 11.2 %copy-start.4 = (bf16[1,5,1,256,128]{4,3,2,1,0:T(8,128)(2,1)S(1)}, bf16[1,5,1,256,128]{4,3,2,1,0:T(8,128)(2,1)}, u32[]{:S(2)}) copy-start(bf16[1,5,1,256,128]{4,3,2,1,0:T(8,128)(2,1)} %get-tuple-element.51) | copy-start | bytes 983044
  47.7 11.2 %copy-start.5 = (bf16[1,5,1,256,128]{4,3,2,1,0:T(8,128)(2,1)S(1)}, bf16[1,5,1,256,128]{4,3,2,1,0:T(8,128)(2,1)}, u32[]{:S(2)}) copy-start(bf16[1,5,1,256,128]{4,3,2,1,0:T(8,128)(2,1)} %get-tuple-element.52) | copy-start | bytes 983044
  47.7 11.2 %copy-start.6 = (bf16[1,5,1,256,128]{4,3,2,1,0:T(8,128)(2,1)S(1)}, bf16[1,5,1,256,128]{4,3,2,1,0:T(8,128)(2,1)}, u32[]{:S(2)}) copy-start(bf16[1,5,1,256,128]{4,3,2,1,0:T(8,128)(2,1)} %get-tuple-element.53) | copy-start | bytes 983044
  49.6 9.3 %copy-start.7 = (bf16[1,5,1,256,128]{4,3,2,1,0:T(8,128)(2,1)S(1)}, bf16[1,5,1,256,128]{4,3,2,1,0:T(8,128)(2,1)}, u32[]{:S(2)}) copy-start(bf16[1,5,1,256,128]{4,3,2,1,0:T(8,128)(2,1)} %get-tuple-element.54) | copy-start | bytes 983044
  49.6 9.3 %copy-start.9 = (bf16[1,5,1,256,128]{4,3,2,1,0:T(8,128)(2,1)S(1)}, bf16[1,5,1,256,128]{4,3,2,1,0:T(8,128)(2,1)}, u32[]{:S(2)}) copy-start(bf16[1,5,1,256,128]{4,3,2,1,0:T(8,128)(2,1)} %get-tuple-element.55) | copy-start | bytes 983044
  49.6 9.3 %copy-start.11 = (bf16[1,5,1,256,128]{4,3,2,1,0:T(8,128)(2,1)S(1)}, bf16[1,5,1,256,128]{4,3,2,1,0:T(8,128)(2,1)}, u32[]{:S(2)}) copy-start(bf16[1,5,1,256,128]{4,3,2,1,0:T(8,128)(2,1)} %get-tuple-element.56) | copy-start | bytes 983044
  49.6 9.3 %copy-start.13 = (bf16[1,5,1,256,128]{4,3,2,1,0:T(8,128)(2,1)S(1)}, bf16[1,5,1,256,128]{4,3,2,1,0:T(8,128)(2,1)}, u32[]{:S(2)}) copy-start(bf16[1,5,1,256,128]{4,3,2,1,0:T(8,128)(2,1)} %get-tuple-element.57) | copy-start | bytes 983044
  49.6 9.4 %copy-start.15 = (bf16[1,5,1,256,128]{4,3,2,1,0:T(8,128)(2,1)S(1)}, bf16[1,5,1,256,128]{4,3,2,1,0:T(8,128)(2,1)}, u32[]{:S(2)}) copy-start(bf16[1,5,1,256,128]{4,3,2,1,0:T(8,128)(2,1)} %get-tuple-element.58) | copy-start | bytes 983044
  49.7 9.4 %copy-start.17 = (bf16[1,5,1,256,128]{4,3,2,1,0:T(8,128)(2,1)S(1)}, bf16[1,5,1,256,128]{4,3,2,1,0:T(8,128)(2,1)}, u32[]{:S(2)}) copy-start(bf16[1,5,1,256,128]{4,3,2,1,0:T(8,128)(2,1)} %get-tuple-element.59) | copy-start | bytes 983044
  49.7 9.4 %copy-start.19 = (bf16[1,5,1,256,128]{4,3,2,1,0:T(8,128)(2,1)S(1)}, bf16[1,5,1,256,128]{4,3,2,1,0:T(8,128)(2,1)}, u32[]{:S(2)}) copy-start(bf16[1,5,1,256,128]{4,3,2,1,0:T(8,128)(2,1)} %get-tuple-element.60) | copy-start | bytes 983044
  59.0 18.2 %copy-start.29 = (f32[1,256,128]{2,1,0:T(8,128)S(1)}, f32[1,256,128]{2,1,0:T(8,128)}, u32[]{:S(2)}) copy-start(f32[1,256,128]{2,1,0:T(8,128)} %copy-done.28) | copy-start | bytes 393220
  59.0 18.2 %copy-start.31 = (f32[1,256,128]{2,1,0:T(8,128)S(1)}, f32[1,256,128]{2,1,0:T(8,128)}, u32[]{:S(2)}) copy-start(f32[1,256,128]{2,1,0:T(8,128)} %copy-done.30) | copy-start | bytes 393220
  59.0 18.2 %copy-start.34 = (f32[8,32,128]{2,0,1:T(8,128)S(1)}, f32[8,32,128]{2,0,1:T(8,128)}, u32[]{:S(2)}) copy-start(f32[8,32,128]{2,0,1:T(8,128)} %copy-done.33) | copy-start | bytes 393220
  59.1 18.2 %copy-start.37 = (f32[8,32,128]{2,0,1:T(8,128)S(1)}, f32[8,32,128]{2,0,1:T(8,128)}, u32[]{:S(2)}) copy-start(f32[8,32,128]{2,0,1:T(8,128)} %copy-done.36) | copy-start | bytes 393220
  59.1 18.2 %copy-start.40 = (f32[8,32,128]{2,0,1:T(8,128)S(1)}, f32[8,32,128]{2,0,1:T(8,128)}, u32[]{:S(2)}) copy-start(f32[8,32,128]{2,0,1:T(8,128)} %copy-done.39) | copy-start | bytes 393220
  59.1 18.2 %copy-start.43 = (f32[8,32,128]{2,0,1:T(8,128)S(1)}, f32[8,32,128]{2,0,1:T(8,128)}, u32[]{:S(2)}) copy-start(f32[8,32,128]{2,0,1:T(8,128)} %copy-done.42) | copy-start | bytes 393220
  59.1 18.2 %copy-start.46 = (f32[8,32,128]{2,0,1:T(8,128)S(1)}, f32[8,32,128]{2,0,1:T(8,128)}, u32[]{:S(2)}) copy-start(f32[8,32,128]{2,0,1:T(8,128)} %copy-done.45) | copy-start | bytes 393220
  59.1 18.2 %copy-start.49 = (f32[1,256,128]{2,1,0:T(8,128)S(1)}, f32[1,256,128]{2,1,0:T(8,128)}, u32[]{:S(2)}) copy-start(f32[1,256,128]{2,1,0:T(8,128)} %copy-done.48) | copy-start | bytes 393220
  59.1 18.2 %copy-start.51 = (f32[1,256,128]{2,1,0:T(8,128)S(1)}, f32[1,256,128]{2,1,0:T(8,128)}, u32[]{:S(2)}) copy-start(f32[1,256,128]{2,1,0:T(8,128)} %copy-done.50) | copy-start | bytes 393220
  59.1 19.0 %copy-start.54 = (f32[8,32,128]{2,0,1:T(8,128)S(1)}, f32[8,32,128]{2,0,1:T(8,128)}, u32[]{:S(2)}) copy-start(f32[8,32,128]{2,0,1:T(8,128)} %copy-done.53) | copy-start | bytes 393220
  59.1 19.0 %copy-start.57 = (f32[8,32,128]{2,0,1:T(8,128)S(1)}, f32[8,32,128]{2,0,1:T(8,128)}, u32[]{:S(2)}) copy-start(f32[8,32,128]{2,0,1:T(8,128)} %copy-done.56) | copy-start | bytes 393220
  59.1 19.0 %copy-start.60 = (f32[8,32,128]{2,0,1:T(8,128)S(1)}, f32[8,32,128]{2,0,1:T(8,128)}, u32[]{:S(2)}) copy-start(f32[8,32,128]{2,0,1:T(8,128)} %copy-done.59) | copy-start | bytes 393220
  59.1 19.0 %copy-start.63 = (f32[1,256,128]{2,1,0:T(8,128)S(1)}, f32[1,256,128]{2,1,0:T(8,128)}, u32[]{:S(2)}) copy-start(f32[1,256,128]{2,1,0:T(8,128)} %copy-done.62) | copy-start | bytes 393220
  59.2 19.0 %copy-start.66 = (f32[1,1,256,128]{3,2,1,0:T(8,128)S(1)}, f32[1,1,256,128]{3,2,1,0:T(8,128)}, u32[]{:S(2)}) copy-start(f32[1,1,256,128]{3,2,1,0:T(8,128)} %copy-done.65) | copy-start | bytes 393220
  59.2 19.0 %copy-start.68 = (f32[8,32,128]{2,0,1:T(8,128)S(1)}, f32[8,32,128]{2,0,1:T(8,128)}, u32[]{:S(2)}) copy-start(f32[8,32,128]{2,0,1:T(8,128)} %get-tuple-element.186) | copy-start | bytes 393220
  59.2 19.0 %copy-start.70 = (f32[8,32,128]{2,0,1:T(8,128)S(1)}, f32[8,32,128]{2,0,1:T(8,128)}, u32[]{:S(2)}) copy-start(f32[8,32,128]{2,0,1:T(8,128)} %get-tuple-element.187) | copy-start | bytes 393220
  59.2 19.0 %copy-start.72 = (f32[8,32,128]{2,0,1:T(8,128)S(1)}, f32[8,32,128]{2,0,1:T(8,128)}, u32[]{:S(2)}) copy-start(f32[8,32,128]{2,0,1:T(8,128)} %get-tuple-element.188) | copy-start | bytes 393220
  59.2 19.0 %copy-start.74 = (f32[8,32,128]{2,0,1:T(8,128)S(1)}, f32[8,32,128]{2,0,1:T(8,128)}, u32[]{:S(2)}) copy-start(f32[8,32,128]{2,0,1:T(8,128)} %get-tuple-element.193) | copy-start | bytes 393220
  59.2 19.0 %copy-start.76 = (f32[8,32,128]{2,0,1:T(8,128)S(1)}, f32[8,32,128]{2,0,1:T(8,128)}, u32[]{:S(2)}) copy-start(f32[8,32,128]{2,0,1:T(8,128)} %get-tuple-element.194) | copy-start | bytes 393220
  59.2 19.0 %copy-start.78 = (f32[8,32,128]{2,0,1:T(8,128)S(1)}, f32[8,32,128]{2,0,1:T(8,128)}, u32[]{:S(2)}) copy-start(f32[8,32,128]{2,0,1:T(8,128)} %get-tuple-element.195) | copy-start | bytes 393220
  59.2 19.0 %copy-start.80 = (f32[8,32,128]{2,0,1:T(8,128)S(1)}, f32[8,32,128]{2,0,1:T(8,128)}, u32[]{:S(2)}) copy-start(f32[8,32,128]{2,0,1:T(8,128)} %get-tuple-element.185) | copy-start | bytes 393220
  59.2 19.0 %copy-start.82 = (f32[8,32,128]{2,0,1:T(8,128)S(1)}, f32[8,32,128]{2,0,1:T(8,128)}, u32[]{:S(2)}) copy-start(f32[8,32,128]{2,0,1:T(8,128)} %get-tuple-element.189) | copy-start | bytes 393220
  59.2 19.0 %copy-start.84 = (f32[8,32,128]{2,0,1:T(8,128)S(1)}, f32[8,32,128]{2,0,1:T(8,128)}, u32[]{:S(2)}) copy-start(f32[8,32,128]{2,0,1:T(8,128)} %get-tuple-element.190) | copy-start | bytes 393220
  59.3 19.0 %copy-start.86 = (f32[8,32,128]{2,0,1:T(8,128)S(1)}, f32[8,32,128]{2,0,1:T(8,128)}, u32[]{:S(2)}) copy-start(f32[8,32,128]{2,0,1:T(8,128)} %get-tuple-element.191) | copy-start | bytes 393220
  59.3 19.0 %copy-start.88 = (f32[8,32,128]{2,0,1:T(8,128)S(1)}, f32[8,32,128]{2,0,1:T(8,128)}, u32[]{:S(2)}) copy-start(f32[8,32,128]{2,0,1:T(8,128)} %get-tuple-element.192) | copy-start | bytes 393220
  59.3 19.0 %copy-start.91 = (f32[1,1,256,128]{3,2,1,0:T(8,128)S(1)}, f32[1,1,256,128]{3,2,1,0:T(8,128)}, u32[]{:S(2)}) copy-start(f32[1,1,256,128]{3,2,1,0:T(8,128)} %copy-done.90) | copy-start | bytes 393220
  80.8 29.3 %copy-start.96 = (pred[2,128]{1,0:T(4,128)(4,1)S(1)}, pred[2,128]{1,0:T(4,128)(4,1)}, u32[]{:S(2)}) copy-start(pred[2,128]{1,0:T(4,128)(4,1)} %and_bitcast_fusion) | copy-start | bytes 772
  83.3 32.2 %copy-start.8 = (bf16[1,5,1,256,128]{4,3,2,1,0:T(8,128)(2,1)S(1)}, bf16[1,5,1,256,128]{4,3,2,1,0:T(8,128)(2,1)}, u32[]{:S(2)}) copy-start(bf16[1,5,1,256,128]{4,3,2,1,0:T(8,128)(2,1)} %get-tuple-element.54) | copy-start | bytes 983044
  83.3 32.2 %copy-start.10 = (bf16[1,5,1,256,128]{4,3,2,1,0:T(8,128)(2,1)S(1)}, bf16[1,5,1,256,128]{4,3,2,1,0:T(8,128)(2,1)}, u32[]{:S(2)}) copy-start(bf16[1,5,1,256,128]{4,3,2,1,0:T(8,128)(2,1)} %get-tuple-element.55) | copy-start | bytes 983044
  83.3 32.2 %copy-start.12 = (bf16[1,5,1,256,128]{4,3,2,1,0:T(8,128)(2,1)S(1)}, bf16[1,5,1,256,128]{4,3,2,1,0:T(8,128)(2,1)}, u32[]{:S(2)}) copy-start(bf16[1,5,1,256,128]{4,3,2,1,0:T(8,128)(2,1)} %get-tuple-element.56) | copy-start | bytes 983044
  83.3 29.7 %collective-permute-start.3 = (f32[5,128]{1,0:T(8,128)S(1)}, f32[5,128]{1,0:T(8,128)S(1)}, u32[]{:S(2)}, u32[]{:S(2)}) collective-permute-start(f32[5,128]{1,0:T(8,128)S(1)} %bitcast.592), channel_id=1, source_target_pairs={{0,15},{1,0},{2,1},{3,2},{4,3},{5,4},{6,5},{7,6},{8,7},{9,8},{10,9... | collective-permute-start | bytes 7688 | tf_op jit(solution)/shard_map/ppermute | solution.py:11
  83.4 29.6 %collective-permute-start.2 = (f32[5,128]{1,0:T(8,128)S(1)}, f32[5,128]{1,0:T(8,128)S(1)}, u32[]{:S(2)}, u32[]{:S(2)}) collective-permute-start(f32[5,128]{1,0:T(8,128)S(1)} %bitcast.590), channel_id=1, source_target_pairs={{0,1},{1,2},{2,3},{3,4},{4,5},{5,6},{6,7},{7,8},{8,9},{9,10},{10,1... | collective-permute-start | bytes 7688 | tf_op jit(solution)/shard_map/ppermute | solution.py:11
  110.1 5.4 %copy-start.16 = (bf16[1,5,1,256,128]{4,3,2,1,0:T(8,128)(2,1)S(1)}, bf16[1,5,1,256,128]{4,3,2,1,0:T(8,128)(2,1)}, u32[]{:S(2)}) copy-start(bf16[1,5,1,256,128]{4,3,2,1,0:T(8,128)(2,1)} %get-tuple-element.58) | copy-start | bytes 983044
  115.6 22.2 %copy-start.52 = (f32[1,256,128]{2,1,0:T(8,128)S(1)}, f32[1,256,128]{2,1,0:T(8,128)}, u32[]{:S(2)}) copy-start(f32[1,256,128]{2,1,0:T(8,128)} %copy-done.50) | copy-start | bytes 393220
  115.6 23.7 %copy-start.32 = (f32[1,256,128]{2,1,0:T(8,128)S(1)}, f32[1,256,128]{2,1,0:T(8,128)}, u32[]{:S(2)}) copy-start(f32[1,256,128]{2,1,0:T(8,128)} %copy-done.30) | copy-start | bytes 393220
  115.6 23.7 %copy-start.35 = (f32[8,32,128]{2,0,1:T(8,128)S(1)}, f32[8,32,128]{2,0,1:T(8,128)}, u32[]{:S(2)}) copy-start(f32[8,32,128]{2,0,1:T(8,128)} %copy-done.33) | copy-start | bytes 393220
  115.6 23.7 %copy-start.38 = (f32[8,32,128]{2,0,1:T(8,128)S(1)}, f32[8,32,128]{2,0,1:T(8,128)}, u32[]{:S(2)}) copy-start(f32[8,32,128]{2,0,1:T(8,128)} %copy-done.36) | copy-start | bytes 393220
  115.6 23.7 %copy-start.41 = (f32[8,32,128]{2,0,1:T(8,128)S(1)}, f32[8,32,128]{2,0,1:T(8,128)}, u32[]{:S(2)}) copy-start(f32[8,32,128]{2,0,1:T(8,128)} %copy-done.39) | copy-start | bytes 393220
  115.6 23.7 %copy-start.44 = (f32[8,32,128]{2,0,1:T(8,128)S(1)}, f32[8,32,128]{2,0,1:T(8,128)}, u32[]{:S(2)}) copy-start(f32[8,32,128]{2,0,1:T(8,128)} %copy-done.42) | copy-start | bytes 393220
  115.7 23.7 %copy-start.47 = (f32[8,32,128]{2,0,1:T(8,128)S(1)}, f32[8,32,128]{2,0,1:T(8,128)}, u32[]{:S(2)}) copy-start(f32[8,32,128]{2,0,1:T(8,128)} %copy-done.45) | copy-start | bytes 393220
  115.7 23.7 %copy-start.64 = (f32[1,256,128]{2,1,0:T(8,128)S(1)}, f32[1,256,128]{2,1,0:T(8,128)}, u32[]{:S(2)}) copy-start(f32[1,256,128]{2,1,0:T(8,128)} %copy-done.62) | copy-start | bytes 393220
  115.7 23.7 %copy-start.83 = (f32[8,32,128]{2,0,1:T(8,128)S(1)}, f32[8,32,128]{2,0,1:T(8,128)}, u32[]{:S(2)}) copy-start(f32[8,32,128]{2,0,1:T(8,128)} %get-tuple-element.189) | copy-start | bytes 393220
  115.7 23.7 %copy-start.85 = (f32[8,32,128]{2,0,1:T(8,128)S(1)}, f32[8,32,128]{2,0,1:T(8,128)}, u32[]{:S(2)}) copy-start(f32[8,32,128]{2,0,1:T(8,128)} %get-tuple-element.190) | copy-start | bytes 393220
  115.7 23.7 %copy-start.87 = (f32[8,32,128]{2,0,1:T(8,128)S(1)}, f32[8,32,128]{2,0,1:T(8,128)}, u32[]{:S(2)}) copy-start(f32[8,32,128]{2,0,1:T(8,128)} %get-tuple-element.191) | copy-start | bytes 393220
  115.7 23.7 %copy-start.89 = (f32[8,32,128]{2,0,1:T(8,128)S(1)}, f32[8,32,128]{2,0,1:T(8,128)}, u32[]{:S(2)}) copy-start(f32[8,32,128]{2,0,1:T(8,128)} %get-tuple-element.192) | copy-start | bytes 393220
  (39 other events, 116.8 us)
where the time goes:
time: 144 us; the launch traced here: 143 us
  other arithmetic  57.9 us (40%)
  blocking collectives  40.1 us (28%)
  local copies, waits for them, and re-layouts  35.2 us (24%)
  starting transfers between devices  6 us (4%)
  between operations  4.3 us (3%)
    all_gather x2, blocking collectives, on_device(): everything = lax.all_gather(edge_pair[None], 'blk', axis=0, tiled=True)  40.1 us
    add x2, other arithmetic, couple(): coupled + off_diag[face, :, component] * neighbours[face][component][None]  39.9 us
    slice x2, local copies, waits for them, and re-layouts, couple(): off_diag[face, :, component] * neighbours[face][component][None]  7.36 us
    gather x4, local copies, waits for them, and re-layouts, on_device(): strips = jnp.take_along_axis(incoming, orders[:, None, :], axis=2)  6.14 us
    ppermute x4, starting transfers between devices, shifted(): lax.ppermute(value, axis, [(i, (i + by) % count) for i in range(count)])  6 us
    slice x2, other arithmetic, couple(): neighbours[face][component][None]  4.47 us
    sub x4, other arithmetic, substitute(): running = running - multipliers[row_at, col_at] * forward[col_at]  3.19 us
    slice x2, local copies, waits for them, and re-layouts, factor(): diag_block[row_at, col_at]  3.14 us
  transfers between devices with their start and end apart: 4, of which 0 were waited for; matrix products, arithmetic and copies ran while one was open for 18% of the time, Pallas kernels for 0%

commit v1 on v0

v1 whole, which is shorter than its diff:
```python
import functools

import jax
import jax.numpy as jnp
from jax import lax
from jax.experimental import pallas as pl
from jax.experimental.pallas import tpu as pltpu
from jax.sharding import PartitionSpec as P

F32 = jnp.float32
VMEM = pltpu.VMEM
TOKEN = 40
A_AT, M_AT, CODE_AT = 5, 10, 35
PLANE = 4
MIB = 2**20


def lu(entries):
    entries = [list(row) for row in entries]
    for pivot_at in range(5):
        inverse = 1.0 / entries[pivot_at][pivot_at]
        for row_at in range(pivot_at + 1, 5):
            scale_now = entries[row_at][pivot_at] * inverse
            entries[row_at][pivot_at] = scale_now
            for col_at in range(pivot_at + 1, 5):
                entries[row_at][col_at] = (
                    entries[row_at][col_at] - scale_now * entries[pivot_at][col_at]
                )
        entries[pivot_at][pivot_at] = inverse
    return entries


def solve(factor_at, vector):
    forward = []
    for row_at in range(5):
        running = vector[row_at]
        for col_at in range(row_at):
            running = running - factor_at(row_at, col_at) * forward[col_at]
        forward.append(running)
    result = [None] * 5
    for row_at in reversed(range(5)):
        running = forward[row_at]
        for col_at in range(row_at + 1, 5):
            running = running - factor_at(row_at, col_at) * result[col_at]
        result[row_at] = running * factor_at(row_at, row_at)
    return result


def south(value, lane):
    return jnp.where(lane == 0, 0.0, pltpu.roll(value, 1, 1))


def north(value, lane):
    return jnp.where(lane == 127, 0.0, pltpu.roll(value, 127, 1))


def outer_face(side):
    return side


def edge_kernel(
    blocks, pairs, rhs_h, off_h, diag_h, token, factors, off_edge, rhs_edge, diag_edge, sems
):
    rows = rhs_h.shape[1]
    copies = []
    for side in range(2):
        at8, at16 = (0, 0) if side == 0 else (rows - 8, rows - 16)
        copies.append(
            (
                pltpu.make_async_copy(
                    diag_h.at[:, :, pl.ds(at8, 8)], diag_edge.at[side], sems.at[side, 0]
                ),
                pltpu.make_async_copy(
                    rhs_h.at[:, pl.ds(at8, 8)], rhs_edge.at[side], sems.at[side, 1]
                ),
                pltpu.make_async_copy(
                    off_h.at[:, :, :, pl.ds(at16, 16)], off_edge.at[side], sems.at[side, 2]
                ),
            )
        )
    for part in range(3):
        for side in range(2):
            copies[side][part].start()
    count = blocks.shape[0]
    me = lax.axis_index("blk")
    before = lax.rem(me + count - 1, count)
    after = lax.rem(me + 1, count)
    first_end = blocks[before] != blocks[me]
    last_end = blocks[after] != blocks[me]
    codes = (
        jnp.where(first_end, jnp.maximum(pairs[0, 0], 0), 2 * before + 1),
        jnp.where(last_end, jnp.maximum(pairs[0, 1], 0), 2 * after),
    )
    lane = lax.broadcasted_iota(jnp.int32, (8, 128), 1)
    for side in range(2):
        for part in range(3):
            copies[side][part].wait()
    for side in range(2):
        edge_row = 0 if side == 0 else 7
        half = slice(0, 8) if side == 0 else slice(8, 16)
        outer, inner = (0, 1) if side == 0 else (1, 0)

        def off(face, a, b):
            return off_edge[side, face, a, b].astype(F32)[half]

        e = lu([[diag_edge[side, a, b] for b in range(5)] for a in range(5)])
        for a in range(5):
            for b in range(5):
                factors[side, 5 * a + b] = e[a][b]
        factor_at = lambda a, b: e[a][b]
        rhs = [rhs_edge[side, a] for a in range(5)]
        u0 = solve(factor_at, rhs)
        acc = list(rhs)
        for b in range(5):
            around = (
                (inner, pltpu.roll(u0[b], 7 if side == 0 else 1, 0)),
                (2, south(u0[b], lane)),
                (3, north(u0[b], lane)),
            )
            for face, value in around:
                for a in range(5):
                    acc[a] = acc[a] - off(face, a, b) * value
        base = solve(factor_at, acc)
        at = TOKEN * side
        for a in range(5):
            token[pl.ds(at + a, 1)] = u0[a][edge_row : edge_row + 1]
            token[pl.ds(at + A_AT + a, 1)] = base[a][edge_row : edge_row + 1]
        for b in range(5):
            column = solve(factor_at, [off(outer, a, b) for a in range(5)])
            for a in range(5):
                token[pl.ds(at + M_AT + 5 * a + b, 1)] = column[a][edge_row : edge_row + 1]
        token[pl.ds(at + CODE_AT, 1)] = jnp.full((1, 128), codes[side], jnp.int32).astype(F32)
        token[pl.ds(at + CODE_AT + 1, TOKEN - CODE_AT - 1)] = jnp.zeros(
            (TOKEN - CODE_AT - 1, 128), F32
        )


def interior_kernel(rhs, off, diag, out_h, edges, factors, now, later, sems):
    rows = rhs.shape[1]
    tile1, tile2 = 32, 64
    for b in range(5):
        for field in (now, later):
            field[b, 0:8] = jnp.zeros((8, 128), F32)
            field[b, 8 + rows : 16 + rows] = jnp.zeros((8, 128), F32)

    def first(step, _):
        at = pl.multiple_of(step * tile1, tile1)
        here = pl.ds(at, tile1)
        e = lu([[diag[a, b, here] for b in range(5)] for a in range(5)])
        for a in range(5):
            for b in range(5):
                factors[a, b, here] = e[a][b]
        u0 = solve(lambda a, b: e[a][b], [rhs[a, here] for a in range(5)])
        for a in range(5):
            now[a, pl.ds(at + 8, tile1)] = u0[a]
        return 0

    lax.fori_loop(0, rows // tile1, first, 0)
    lane = lax.broadcasted_iota(jnp.int32, (tile2, 128), 1)
    for source, target in ((now, later), (later, now)):

        def sweep(step, _):
            at = pl.multiple_of(step * tile2, tile2)
            here = pl.ds(at, tile2)
            acc = [rhs[a, here] for a in range(5)]
            for b in range(5):
                middle = source[b, pl.ds(at + 8, tile2)]
                around = (
                    source[b, pl.ds(at + 7, tile2)],
                    source[b, pl.ds(at + 9, tile2)],
                    south(middle, lane),
                    north(middle, lane),
                )
                for face in range(4):
                    for a in range(5):
                        acc[a] = acc[a] - off[face, a, b, here].astype(F32) * around[face]
            fresh = solve(lambda a, b: factors[a, b, here], acc)
            for a in range(5):
                target[a, pl.ds(at + 8, tile2)] = fresh[a]
            return 0

        lax.fori_loop(0, rows // tile2, sweep, 0)
    copy = pltpu.make_async_copy(now.at[:, pl.ds(8, rows)], out_h, sems.at[0])
    copy.start()
    for a in range(5):
        edges[0, a] = now[a, 8:16]
        edges[1, a] = now[a, rows : rows + 8]
    copy.wait()


def select_kernel(*refs):
    lines = len(refs) - PLANE
    tokens, outs = refs[:lines], refs[lines:]
    me = lax.axis_index("blk")
    for other in range(PLANE):
        for slot in range(2):
            wanted = (2 * (me ^ other) + slot).astype(F32)
            found = jnp.zeros((TOKEN, 128), F32)
            for token in tokens:
                for side in range(2):
                    code = token[pl.ds(TOKEN * side + CODE_AT, 1)]
                    value = token[pl.ds(TOKEN * side, TOKEN)]
                    found = jnp.where(code == wanted, value, found)
            outs[other][pl.ds(TOKEN * slot, TOKEN)] = found


def finish_kernel(*refs):
    out_in, own, *arrived = refs[: 2 + PLANE]
    order, off_edge, factors, edges, out_h, beyond, result, sems = refs[2 + PLANE :]
    rows = out_h.shape[1]
    me = lax.axis_index("blk")
    lane = lax.broadcasted_iota(jnp.int32, (8, 128), 1)
    row = lax.broadcasted_iota(jnp.int32, (8, 128), 0)
    copies = []
    for side in range(2):
        at = TOKEN * side
        half = slice(0, 8) if side == 0 else slice(8, 16)
        edge_row, next_row = (0, 1) if side == 0 else (7, 6)
        outer = outer_face(side)
        source = own[pl.ds(at + CODE_AT, 1)].astype(jnp.int32) // 2
        found = arrived[0][pl.ds(at, TOKEN)]
        for other in range(1, PLANE):
            here = lax.rem(source, PLANE) == ((me ^ other) % PLANE)
            found = jnp.where(here, arrived[other][pl.ds(at, TOKEN)], found)
        columns = jnp.broadcast_to(order[0, side : side + 1], (TOKEN, 128))
        beyond[side] = jnp.take_along_axis(found, columns, axis=1)

        def mine(k):
            return own[pl.ds(at + k, 1)]

        def theirs(k):
            return beyond[side, pl.ds(k, 1)]

        def off(face, a, b):
            return off_edge[side, face, a, b].astype(F32)[half]

        acc = [jnp.zeros((8, 128), F32) for _ in range(5)]
        ahead, change = [], []
        for a in range(5):
            u1, delta = theirs(A_AT + a), jnp.zeros((1, 128), F32)
            for b in range(5):
                u1 = u1 - theirs(M_AT + 5 * a + b) * mine(b)
                delta = delta - mine(M_AT + 5 * a + b) * theirs(b)
            ahead.append(jnp.broadcast_to(u1, (8, 128)))
            change.append(jnp.broadcast_to(delta, (8, 128)))
        for b in range(5):
            at_edge = row == edge_row
            around = (
                (outer, jnp.where(at_edge, ahead[b], jnp.where(row == next_row, change[b], 0.0))),
                (2, jnp.where(at_edge, south(change[b], lane), 0.0)),
                (3, jnp.where(at_edge, north(change[b], lane), 0.0)),
            )
            for face, value in around:
                for a in range(5):
                    acc[a] = acc[a] + off(face, a, b) * value
        less = solve(lambda a, b: factors[side, 5 * a + b], acc)
        for a in range(5):
            result[side, a] = edges[side, a] - less[a]
        copies.append(
            pltpu.make_async_copy(
                result.at[side],
                out_h.at[:, pl.ds(0 if side == 0 else rows - 8, 8)],
                sems.at[side],
            )
        )
        copies[-1].start()
    for copy in copies:
        copy.wait()


def in_vmem(value):
    return pltpu.with_memory_space_constraint(value, VMEM)


def in_hbm(value):
    return pltpu.with_memory_space_constraint(value, pltpu.HBM)


def crossed(value, by):
    count = lax.axis_size("blk")
    return lax.ppermute(value, "blk", [(i, i ^ by) for i in range(count)])


def on_device(right_side, off_diag, diag_block, block_of_device, interface_pairs, strip_order):
    count = lax.axis_size("blk")
    rows = right_side.shape[1]
    any_space = pl.BlockSpec(memory_space=pl.ANY)
    in_smem = pl.BlockSpec(memory_space=pltpu.SMEM)
    whole = pl.BlockSpec(memory_space=VMEM)
    token, factors_edge, off_edge = pl.pallas_call(
        edge_kernel,
        out_shape=(
            VMEM((2 * TOKEN, 128), F32),
            VMEM((2, 25, 8, 128), F32),
            VMEM((2, 4, 5, 5, 16, 128), off_diag.dtype),
        ),
        in_specs=[in_smem, in_smem, any_space, any_space, any_space],
        out_specs=(whole, whole, whole),
        scratch_shapes=[
            VMEM((2, 5, 8, 128), F32),
            VMEM((2, 5, 5, 8, 128), F32),
            pltpu.SemaphoreType.DMA((2, 3)),
        ],
        compiler_params=pltpu.CompilerParams(vmem_limit_bytes=8 * MIB),
        name="edges",
    )(block_of_device, interface_pairs, in_hbm(right_side), in_hbm(off_diag), in_hbm(diag_block))

    lines = count // PLANE
    if lines <= 8:
        tokens = [token] + [crossed(token, PLANE * k) for k in range(1, lines)]
    else:
        groups = [[PLANE * k + j for k in range(lines)] for j in range(PLANE)]
        gathered = lax.all_gather(token, "blk", axis_index_groups=groups)
        tokens = [gathered[k] for k in range(lines)]

    inside, edges = pl.pallas_call(
        interior_kernel,
        out_shape=(pltpu.HBM(right_side.shape, F32), VMEM((2, 5, 8, 128), F32)),
        in_specs=[whole, whole, whole],
        out_specs=(any_space, whole),
        scratch_shapes=[
            VMEM((5, 5, rows, 128), F32),
            VMEM((5, rows + 16, 128), F32),
            VMEM((5, rows + 16, 128), F32),
            pltpu.SemaphoreType.DMA((1,)),
        ],
        compiler_params=pltpu.CompilerParams(vmem_limit_bytes=16 * MIB),
        cost_estimate=pl.CostEstimate(
            flops=32000000, bytes_accessed=12 * MIB, transcendentals=0
        ),
        name="interior",
    )(in_vmem(right_side), in_vmem(off_diag), in_vmem(diag_block))

    chosen = pl.pallas_call(
        select_kernel,
        out_shape=[VMEM((2 * TOKEN, 128), F32)] * PLANE,
        in_specs=[whole] * len(tokens),
        out_specs=[whole] * PLANE,
        compiler_params=pltpu.CompilerParams(vmem_limit_bytes=8 * MIB),
        name="choose",
    )(*[in_vmem(value) for value in tokens])
    arrived = [chosen[0]] + [crossed(chosen[k], k) for k in range(1, PLANE)]

    return pl.pallas_call(
        finish_kernel,
        out_shape=pltpu.HBM(right_side.shape, F32),
        in_specs=[any_space] + [whole] * (1 + PLANE + 4),
        out_specs=any_space,
        scratch_shapes=[
            VMEM((2, TOKEN, 128), F32),
            VMEM((2, 5, 8, 128), F32),
            pltpu.SemaphoreType.DMA((2,)),
        ],
        input_output_aliases={0: 0},
        compiler_params=pltpu.CompilerParams(vmem_limit_bytes=8 * MIB),
        name="finish",
    )(
        in_hbm(inside),
        in_vmem(token),
        *[in_vmem(value) for value in arrived],
        strip_order,
        in_vmem(off_edge),
        in_vmem(factors_edge),
        in_vmem(edges),
    )


def solution(mesh):
    return jax.shard_map(
        on_device,
        mesh=mesh,
        in_specs=(
            P(None, ("parts", "blk"), None),
            P(None, None, None, ("parts", "blk"), None),
            P(None, None, ("parts", "blk"), None),
            P(),
            P("blk", None),
            P("blk", None, None),
        ),
        out_specs=P(None, ("parts", "blk"), None),
        check_vma=False,
    )
```

time: 144 us -> 23 us (0.16)
  other arithmetic: 57.9 us -> 0 us
  blocking collectives: 40.1 us -> 0 us
  local copies, waits for them, and re-layouts: 35.2 us -> 1.87 us
  Pallas kernels: 0 us -> 8.91 us
  waiting for transfers between devices: 0.01 us -> 4.27 us
  between operations: 4.3 us -> 0.08 us
  starting transfers between devices: 6 us -> 7.69 us
    all_gather x2 -> x0, blocking collectives: 40.1 us -> none  [on_device(): everything = lax.all_gather(edge_pair[None], 'blk', axis=0, tiled=True)]
    add x2 -> x0, other arithmetic: 39.9 us -> none  [couple(): coupled + off_diag[face, :, component] * neighbours[face][component][None]]
    slice x11 -> x0, local copies, waits for them, and re-layouts: 17.6 us -> none  [the longest x2 7.36 us: couple(): off_diag[face, :, component] * neighbours[face][component][None]]
    gather x8 -> x0, local copies, waits for them, and re-layouts: 9.06 us -> none  [the longest x4 6.14 us: on_device(): strips = jnp.take_along_axis(incoming, orders[:, None, :], axis=2)]
    pallas_call x0 -> x4, Pallas kernels: none -> 8.91 us  [the longest x1 5.16 us: on_device(): pl.pallas_call(interior_kernel, out_shape=(pltpu.HBM(right_side.shape, F3...]
    sub x7 -> x0, other arithmetic: 5.06 us -> none  [the longest x4 3.19 us: substitute(): running = running - multipliers[row_at, col_at] * forward[col_at]]
    slice x2 -> x0, other arithmetic: 4.47 us -> none  [couple(): neighbours[face][component][None]]
    ppermute x4 -> x6, waiting for transfers between devices: 0.01 us -> 4.27 us  [crossed(): return lax.ppermute(value, 'blk', [(i, i ^ by) for i in range(count)])]
  transfers between devices with their start and end apart: 4 -> 6, of which waited for: 0 -> 2; matrix products, arithmetic and copies ran while one was open for 18% -> 0% of each run, Pallas kernels for 0% -> 23%
where the time goes in v1:
time: 23 us; the launch traced here: 22.8 us
  Pallas kernels  8.91 us (39%)
  starting transfers between devices  7.69 us (33%)
  waiting for transfers between devices  4.27 us (19%)
  local copies, waits for them, and re-layouts  1.87 us (8%)
    ppermute x6, starting transfers between devices, crossed(): return lax.ppermute(value, 'blk', [(i, i ^ by) for i in range(count)])  7.69 us
    pallas_call x1, Pallas kernels, on_device(): pl.pallas_call(interior_kernel, out_shape=(pltpu.HBM(right_side.shape, F3...  5.16 us
    ppermute x6, waiting for transfers between devices, crossed(): return lax.ppermute(value, 'blk', [(i, i ^ by) for i in range(count)])  4.27 us
    pallas_call x1, Pallas kernels, on_device(): pl.pallas_call(edge_kernel, out_shape=(VMEM((2 * TOKEN, 128), F32), VMEM(...  2.77 us
    unnamed x12, local copies, waits for them, and re-layouts  1.87 us
    pallas_call x1, Pallas kernels, on_device(): pl.pallas_call(finish_kernel, out_shape=pltpu.HBM(right_side.shape, F32),...  0.89 us
  transfers between devices with their start and end apart: 6, of which 2 were waited for; matrix products, arithmetic and copies ran while one was open for 0% of the time, Pallas kernels for 23%

profile of v1, /device:TPU:0, one launch (start us, length us, event | category | flops | bytes accessed | tf_op | source)
XLA Modules:
  0.0 22.8 jit_solution(18079723646673401355)
XLA Ops:
  0.0 0.0 copy-start.1
  0.0 0.0 copy-start
  0.0 0.0 copy-start.2
  0.0 0.0 copy-start.4
  0.0 0.8 %copy-done.4 = s32[16]{0:T(128)S(1)} copy-done((s32[16]{0:T(128)S(1)}, s32[16]{0:T(128)}, u32[]{:S(2)}) %copy-start.4) | copy-done | bytes 88
  0.8 0.0 copy-start.5
  0.8 1.1 %copy-done.5 = s32[1,2]{1,0:T(1,128)S(1)} copy-done((s32[1,2]{1,0:T(1,128)S(1)}, s32[1,2]{1,0:T(1,128)}, u32[]{:S(2)}) %copy-start.5) | copy-done | bytes 32
  1.9 2.8 %edges.1 = (f32[80,128]{1,0:T(8,128)S(1)}, f32[2,25,8,128]{3,2,1,0:T(8,128)S(1)}, bf16[2,4,5,5,16,128]{5,4,3,2,1,0:T(8,128)(2,1)S(1)}) custom-call(s32[16]{0:T(128)S(1)} %copy-done.4, s32[1,2]{1,0:T(1,128)S(1)} %copy-done.5, f32[5,256,128]{2,1,0:T(8,128)} %rhs_h.1, bf16[4,5,5,256,128]{4,3,2,1,0:T(8,128)(2,1)} %off_h.1, f32[5,5,256,128]{3,2,1,0:T(8,128)} %diag_h.1), custom_call_target="tpu_custom_call" | custom-call | tf_op jit(solution)/shard_map/edges/pallas_call | solution.py:290
  4.6 0.0 copy-start.3
  4.7 5.1 %collective-permute-start.2 = (f32[80,128]{1,0:T(8,128)S(1)}, f32[80,128]{1,0:T(8,128)S(1)}, u32[]{:S(2)}, u32[]{:S(2)}) collective-permute-start(f32[80,128]{1,0:T(8,128)S(1)} %get-tuple-element.15.refs_0_.refs_1_), channel_id=1, source_target_pairs={{0,12},{1,13},{2,14},{3,15},{4,8},{5,9},{6,10},{7,11},{8,4},{9,5},... | collective-permute-start | bytes 122888 | tf_op jit(solution)/shard_map/ppermute | solution.py:281
  9.8 0.0 collective-permute-start.1
  9.8 0.6 %collective-permute-start = (f32[80,128]{1,0:T(8,128)S(1)}, f32[80,128]{1,0:T(8,128)S(1)}, u32[]{:S(2)}, u32[]{:S(2)}) collective-permute-start(f32[80,128]{1,0:T(8,128)S(1)} %get-tuple-element.15.refs_0_.refs_1_), channel_id=1, source_target_pairs={{0,4},{1,5},{2,6},{3,7},{4,0},{5,1},{6,2},{7,3},{8,12},{9,13},{10,... | collective-permute-start | bytes 122888 | tf_op jit(solution)/shard_map/ppermute | solution.py:281
  10.4 1.4 %collective-permute-done.2.refs_3_ = f32[80,128]{1,0:T(8,128)S(1)} collective-permute-done((f32[80,128]{1,0:T(8,128)S(1)}, f32[80,128]{1,0:T(8,128)S(1)}, u32[]{:S(2)}, u32[]{:S(2)}) %collective-permute-start.2) | collective-permute-done | bytes 40992 | tf_op jit(solution)/shard_map/ppermute | solution.py:281
  11.8 2.9 %collective-permute-done.1.refs_2_ = f32[80,128]{1,0:T(8,128)S(1)} collective-permute-done((f32[80,128]{1,0:T(8,128)S(1)}, f32[80,128]{1,0:T(8,128)S(1)}, u32[]{:S(2)}, u32[]{:S(2)}) %collective-permute-start.1) | collective-permute-done | bytes 40992 | tf_op jit(solution)/shard_map/ppermute | solution.py:281
  14.7 0.0 collective-permute-done.refs_1_
  14.7 0.1 choose.1
  14.8 0.1 collective-permute-start.3
  14.8 1.6 %collective-permute-start.4 = (f32[80,128]{1,0:T(8,128)S(1)}, f32[80,128]{1,0:T(8,128)S(1)}, u32[]{:S(2)}, u32[]{:S(2)}) collective-permute-start(f32[80,128]{1,0:T(8,128)S(1)} %get-tuple-element.18), channel_id=1, source_target_pairs={{0,2},{1,3},{2,0},{3,1},{4,6},{5,7},{6,4},{7,5},{8,10},{9,11},{10,... | collective-permute-start | bytes 122888 | tf_op jit(solution)/shard_map/ppermute | solution.py:281
  16.4 0.3 %collective-permute-start.5 = (f32[80,128]{1,0:T(8,128)S(1)}, f32[80,128]{1,0:T(8,128)S(1)}, u32[]{:S(2)}, u32[]{:S(2)}) collective-permute-start(f32[80,128]{1,0:T(8,128)S(1)} %get-tuple-element.19), channel_id=1, source_target_pairs={{0,3},{1,2},{2,1},{3,0},{4,7},{5,6},{6,5},{7,4},{8,11},{9,10},{10,... | collective-permute-start | bytes 122888 | tf_op jit(solution)/shard_map/ppermute | solution.py:281
  16.7 0.0 copy-done.1
  16.7 0.0 copy-done
  16.7 0.0 copy-done.2
  16.7 5.2 %interior.1 = (f32[5,256,128]{2,1,0:T(8,128)}, f32[2,5,8,128]{3,2,1,0:T(8,128)S(1)}) custom-call(f32[5,256,128]{2,1,0:T(8,128)S(1)} %copy-done.2, bf16[4,5,5,256,128]{4,3,2,1,0:T(8,128)(2,1)S(1)} %copy-done, f32[5,5,256,128]{3,2,1,0:T(8,128)S(1)} %copy-done.1), custom_call_target="tpu_custom_call" | custom-call | flops 32000000 | bytes 12582912 | tf_op jit(solution)/shard_map/interior/pallas_call | solution.py:316
  21.9 0.0 collective-permute-done.3.refs_3_
  21.9 0.0 collective-permute-done.4.refs_4_
  21.9 0.0 collective-permute-done.5.refs_5_
  21.9 0.0 copy-done.3
  21.9 0.9 %finish.1 = f32[5,256,128]{2,1,0:T(8,128)} custom-call(f32[5,256,128]{2,1,0:T(8,128)} %get-tuple-element.14.refs_0_, f32[80,128]{1,0:T(8,128)S(1)} %get-tuple-element.15.refs_0_.refs_1_, f32[80,128]{1,0:T(8,128)S(1)} %get-tuple-element.16.refs_2_, f32[80,128]{1,0:T(8,128)S(1)} %collective-permute-done.3.refs_3_, ...), custom_call_target="tpu_custom_call", output_to_operand_aliasing={{}: (0, {})} | custom-call | tf_op jit(solution)/shard_map/finish/pallas_call | solution.py:344
Async XLA Ops:
  0.0 16.7 %copy-start.1 = (f32[5,5,256,128]{3,2,1,0:T(8,128)S(1)}, f32[5,5,256,128]{3,2,1,0:T(8,128)}, u32[]{:S(2)}) copy-start(f32[5,5,256,128]{3,2,1,0:T(8,128)} %diag_h.1) | copy-start | bytes 9830404
  0.0 16.7 %copy-start = (bf16[4,5,5,256,128]{4,3,2,1,0:T(8,128)(2,1)S(1)}, bf16[4,5,5,256,128]{4,3,2,1,0:T(8,128)(2,1)}, u32[]{:S(2)}) copy-start(bf16[4,5,5,256,128]{4,3,2,1,0:T(8,128)(2,1)} %off_h.1) | copy-start | bytes 19660804
  0.0 16.7 %copy-start.2 = (f32[5,256,128]{2,1,0:T(8,128)S(1)}, f32[5,256,128]{2,1,0:T(8,128)}, u32[]{:S(2)}) copy-start(f32[5,256,128]{2,1,0:T(8,128)} %rhs_h.1) | copy-start | bytes 1966084
  0.0 0.8 %copy-start.4 = (s32[16]{0:T(128)S(1)}, s32[16]{0:T(128)}, u32[]{:S(2)}) copy-start(s32[16]{0:T(128)} %blocks.1) | copy-start | bytes 196
  0.8 1.1 %copy-start.5 = (s32[1,2]{1,0:T(1,128)S(1)}, s32[1,2]{1,0:T(1,128)}, u32[]{:S(2)}) copy-start(s32[1,2]{1,0:T(1,128)} %pairs.1) | copy-start | bytes 28
  4.6 17.3 %copy-start.3 = (s32[1,2,128]{2,1,0:T(2,128)S(1)}, s32[1,2,128]{2,1,0:T(2,128)}, u32[]{:S(2)}) copy-start(s32[1,2,128]{2,1,0:T(2,128)} %refs_6_.1) | copy-start | bytes 3076
  4.7 7.1 %collective-permute-start.2 = (f32[80,128]{1,0:T(8,128)S(1)}, f32[80,128]{1,0:T(8,128)S(1)}, u32[]{:S(2)}, u32[]{:S(2)}) collective-permute-start(f32[80,128]{1,0:T(8,128)S(1)} %get-tuple-element.15.refs_0_.refs_1_), channel_id=1, source_target_pairs={{0,12},{1,13},{2,14},{3,15},{4,8},{5,9},{6,10},{7,11},{8,4},{9,5},... | collective-permute-start | bytes 122888 | tf_op jit(solution)/shard_map/ppermute | solution.py:281
  9.8 4.9 %collective-permute-start.1 = (f32[80,128]{1,0:T(8,128)S(1)}, f32[80,128]{1,0:T(8,128)S(1)}, u32[]{:S(2)}, u32[]{:S(2)}) collective-permute-start(f32[80,128]{1,0:T(8,128)S(1)} %get-tuple-element.15.refs_0_.refs_1_), channel_id=1, source_target_pairs={{0,8},{1,9},{2,10},{3,11},{4,12},{5,13},{6,14},{7,15},{8,0},{9,1},... | collective-permute-start | bytes 122888 | tf_op jit(solution)/shard_map/ppermute | solution.py:281
  9.8 4.9 %collective-permute-start = (f32[80,128]{1,0:T(8,128)S(1)}, f32[80,128]{1,0:T(8,128)S(1)}, u32[]{:S(2)}, u32[]{:S(2)}) collective-permute-start(f32[80,128]{1,0:T(8,128)S(1)} %get-tuple-element.15.refs_0_.refs_1_), channel_id=1, source_target_pairs={{0,4},{1,5},{2,6},{3,7},{4,0},{5,1},{6,2},{7,3},{8,12},{9,13},{10,... | collective-permute-start | bytes 122888 | tf_op jit(solution)/shard_map/ppermute | solution.py:281
  14.8 7.1 %collective-permute-start.3 = (f32[80,128]{1,0:T(8,128)S(1)}, f32[80,128]{1,0:T(8,128)S(1)}, u32[]{:S(2)}, u32[]{:S(2)}) collective-permute-start(f32[80,128]{1,0:T(8,128)S(1)} %get-tuple-element.17), channel_id=1, source_target_pairs={{0,1},{1,0},{2,3},{3,2},{4,5},{5,4},{6,7},{7,6},{8,9},{9,8},{10,11... | collective-permute-start | bytes 122888 | tf_op jit(solution)/shard_map/ppermute | solution.py:281
  14.8 7.1 %collective-permute-start.4 = (f32[80,128]{1,0:T(8,128)S(1)}, f32[80,128]{1,0:T(8,128)S(1)}, u32[]{:S(2)}, u32[]{:S(2)}) collective-permute-start(f32[80,128]{1,0:T(8,128)S(1)} %get-tuple-element.18), channel_id=1, source_target_pairs={{0,2},{1,3},{2,0},{3,1},{4,6},{5,7},{6,4},{7,5},{8,10},{9,11},{10,... | collective-permute-start | bytes 122888 | tf_op jit(solution)/shard_map/ppermute | solution.py:281
  16.4 5.5 %collective-permute-start.5 = (f32[80,128]{1,0:T(8,128)S(1)}, f32[80,128]{1,0:T(8,128)S(1)}, u32[]{:S(2)}, u32[]{:S(2)}) collective-permute-start(f32[80,128]{1,0:T(8,128)S(1)} %get-tuple-element.19), channel_id=1, source_target_pairs={{0,3},{1,2},{2,1},{3,0},{4,7},{5,6},{6,5},{7,4},{8,11},{9,10},{10,... | collective-permute-start | bytes 122888 | tf_op jit(solution)/shard_map/ppermute | solution.py:281

commit v2 on v1

--- a/solution.py
+++ b/solution.py
@@ -13,6 +13,9 @@
 A_AT, M_AT, CODE_AT = 5, 10, 35
 PLANE = 4
 MIB = 2**20
+FACTOR_TILE, TILE = 32, 64
+LINE_ORDER = (2, 3, 1)
+PLANE_ORDER = (3, 2, 1)
 
 
 def lu(entries):
@@ -59,9 +62,26 @@
 
 
 def edge_kernel(
-    blocks, pairs, rhs_h, off_h, diag_h, token, factors, off_edge, rhs_edge, diag_edge, sems
+    blocks_h,
+    pairs_h,
+    rhs_h,
+    off_h,
+    diag_h,
+    token,
+    factors,
+    off_edge,
+    blocks,
+    pairs,
+    rhs_edge,
+    diag_edge,
+    sems,
+    scalar_sems,
 ):
     rows = rhs_h.shape[1]
+    scalars = (
+        pltpu.make_async_copy(blocks_h, blocks, scalar_sems.at[0]),
+        pltpu.make_async_copy(pairs_h, pairs, scalar_sems.at[1]),
+    )
     copies = []
     for side in range(2):
         at8, at16 = (0, 0) if side == 0 else (rows - 8, rows - 16)
@@ -81,6 +101,10 @@
     for part in range(3):
         for side in range(2):
             copies[side][part].start()
+    for copy in scalars:
+        copy.start()
+    for copy in scalars:
+        copy.wait()
     count = blocks.shape[0]
     me = lax.axis_index("blk")
     before = lax.rem(me + count - 1, count)
@@ -135,62 +159,87 @@
         )
 
 
-def interior_kernel(rhs, off, diag, out_h, edges, factors, now, later, sems):
+def sweep_rows(source, rhs, off, factors, at, tile):
+    lane = lax.broadcasted_iota(jnp.int32, (tile, 128), 1)
+    here = pl.ds(at, tile)
+    acc = [rhs[a, here] for a in range(5)]
+    for b in range(5):
+        middle = source[b, pl.ds(at + 8, tile)]
+        around = (
+            source[b, pl.ds(at + 7, tile)],
+            source[b, pl.ds(at + 9, tile)],
+            south(middle, lane),
+            north(middle, lane),
+        )
+        for face in range(4):
+            for a in range(5):
+                acc[a] = acc[a] - off[face, a, b, here].astype(F32) * around[face]
+    return solve(lambda a, b: factors[a, b, here], acc)
+
+
+def early_kernel(token, rhs, off, diag, factors, first_sweep, upper, start):
+    del token
     rows = rhs.shape[1]
-    tile1, tile2 = 32, 64
     for b in range(5):
-        for field in (now, later):
+        for field in (start, first_sweep):
             field[b, 0:8] = jnp.zeros((8, 128), F32)
             field[b, 8 + rows : 16 + rows] = jnp.zeros((8, 128), F32)
 
-    def first(step, _):
-        at = pl.multiple_of(step * tile1, tile1)
-        here = pl.ds(at, tile1)
+    def factor_step(step, _):
+        at = pl.multiple_of(step * FACTOR_TILE, FACTOR_TILE)
+        here = pl.ds(at, FACTOR_TILE)
         e = lu([[diag[a, b, here] for b in range(5)] for a in range(5)])
         for a in range(5):
             for b in range(5):
                 factors[a, b, here] = e[a][b]
         u0 = solve(lambda a, b: e[a][b], [rhs[a, here] for a in range(5)])
         for a in range(5):
-            now[a, pl.ds(at + 8, tile1)] = u0[a]
+            start[a, pl.ds(at + 8, FACTOR_TILE)] = u0[a]
         return 0
 
-    lax.fori_loop(0, rows // tile1, first, 0)
-    lane = lax.broadcasted_iota(jnp.int32, (tile2, 128), 1)
-    for source, target in ((now, later), (later, now)):
-
-        def sweep(step, _):
-            at = pl.multiple_of(step * tile2, tile2)
-            here = pl.ds(at, tile2)
-            acc = [rhs[a, here] for a in range(5)]
-            for b in range(5):
-                middle = source[b, pl.ds(at + 8, tile2)]
-                around = (
-                    source[b, pl.ds(at + 7, tile2)],
-                    source[b, pl.ds(at + 9, tile2)],
-                    south(middle, lane),
-                    north(middle, lane),
-                )
-                for face in range(4):
-                    for a in range(5):
-                        acc[a] = acc[a] - off[face, a, b, here].astype(F32) * around[face]
-            fresh = solve(lambda a, b: factors[a, b, here], acc)
-            for a in range(5):
-                target[a, pl.ds(at + 8, tile2)] = fresh[a]
-            return 0
-
-        lax.fori_loop(0, rows // tile2, sweep, 0)
-    copy = pltpu.make_async_copy(now.at[:, pl.ds(8, rows)], out_h, sems.at[0])
-    copy.start()
-    for a in range(5):
-        edges[0, a] = now[a, 8:16]
-        edges[1, a] = now[a, rows : rows + 8]
-    copy.wait()
+    def first_step(step, _):
+        at = pl.multiple_of(step * TILE, TILE)
+        fresh = sweep_rows(start, rhs, off, factors, at, TILE)
+        for a in range(5):
+            first_sweep[a, pl.ds(at + 8, TILE)] = fresh[a]
+        return 0
+
+    def second_step(step, _):
+        at = pl.multiple_of(step * TILE, TILE)
+        fresh = sweep_rows(first_sweep, rhs, off, factors, at, TILE)
+        for a in range(5):
+            upper[a, pl.ds(at, TILE)] = fresh[a]
+        return 0
+
+    lax.fori_loop(0, rows // FACTOR_TILE, factor_step, 0)
+    lax.fori_loop(0, rows // TILE, first_step, 0)
+    lax.fori_loop(0, upper.shape[1] // TILE, second_step, 0)
+
+
+def late_kernel(rhs, off, factors, first_sweep, upper, out_h, lower, sems):
+    done, left = upper.shape[1], lower.shape[1]
+    copies = (
+        pltpu.make_async_copy(upper, out_h.at[:, pl.ds(0, done)], sems.at[0]),
+        pltpu.make_async_copy(lower, out_h.at[:, pl.ds(done, left)], sems.at[1]),
+    )
+    copies[0].start()
+
+    def second_step(step, _):
+        at = pl.multiple_of(step * TILE, TILE)
+        fresh = sweep_rows(first_sweep, rhs, off, factors, done + at, TILE)
+        for a in range(5):
+            lower[a, pl.ds(at, TILE)] = fresh[a]
+        return 0
+
+    lax.fori_loop(0, left // TILE, second_step, 0)
+    copies[1].start()
+    for copy in copies:
+        copy.wait()
 
 
 def select_kernel(*refs):
-    lines = len(refs) - PLANE
-    tokens, outs = refs[:lines], refs[lines:]
+    lines = len(refs) - PLANE - 1
+    tokens, outs = refs[:lines], refs[lines + 1 :]
     me = lax.axis_index("blk")
     for other in range(PLANE):
         for slot in range(2):
@@ -206,7 +255,7 @@
 
 def finish_kernel(*refs):
     out_in, own, *arrived = refs[: 2 + PLANE]
-    order, off_edge, factors, edges, out_h, beyond, result, sems = refs[2 + PLANE :]
+    order, off_edge, factors, upper, lower, out_h, beyond, result, sems = refs[2 + PLANE :]
     rows = out_h.shape[1]
     me = lax.axis_index("blk")
     lane = lax.broadcasted_iota(jnp.int32, (8, 128), 1)
@@ -219,9 +268,9 @@
         outer = outer_face(side)
         source = own[pl.ds(at + CODE_AT, 1)].astype(jnp.int32) // 2
         found = arrived[0][pl.ds(at, TOKEN)]
-        for other in range(1, PLANE):
+        for value, other in zip(arrived[1:], PLANE_ORDER):
             here = lax.rem(source, PLANE) == ((me ^ other) % PLANE)
-            found = jnp.where(here, arrived[other][pl.ds(at, TOKEN)], found)
+            found = jnp.where(here, value[pl.ds(at, TOKEN)], found)
         columns = jnp.broadcast_to(order[0, side : side + 1], (TOKEN, 128))
         beyond[side] = jnp.take_along_axis(found, columns, axis=1)
 
@@ -255,7 +304,8 @@
                     acc[a] = acc[a] + off(face, a, b) * value
         less = solve(lambda a, b: factors[side, 5 * a + b], acc)
         for a in range(5):
-            result[side, a] = edges[side, a] - less[a]
+            near = upper[a, 0:8] if side == 0 else lower[a, pl.ds(lower.shape[1] - 8, 8)]
+            result[side, a] = near - less[a]
         copies.append(
             pltpu.make_async_copy(
                 result.at[side],
@@ -285,7 +335,6 @@
     count = lax.axis_size("blk")
     rows = right_side.shape[1]
     any_space = pl.BlockSpec(memory_space=pl.ANY)
-    in_smem = pl.BlockSpec(memory_space=pltpu.SMEM)
     whole = pl.BlockSpec(memory_space=VMEM)
     token, factors_edge, off_edge = pl.pallas_call(
         edge_kernel,
@@ -294,57 +343,83 @@
             VMEM((2, 25, 8, 128), F32),
             VMEM((2, 4, 5, 5, 16, 128), off_diag.dtype),
         ),
-        in_specs=[in_smem, in_smem, any_space, any_space, any_space],
+        in_specs=[any_space] * 5,
         out_specs=(whole, whole, whole),
         scratch_shapes=[
+            pltpu.SMEM(block_of_device.shape, jnp.int32),
+            pltpu.SMEM(interface_pairs.shape, jnp.int32),
             VMEM((2, 5, 8, 128), F32),
             VMEM((2, 5, 5, 8, 128), F32),
             pltpu.SemaphoreType.DMA((2, 3)),
+            pltpu.SemaphoreType.DMA((2,)),
         ],
         compiler_params=pltpu.CompilerParams(vmem_limit_bytes=8 * MIB),
         name="edges",
-    )(block_of_device, interface_pairs, in_hbm(right_side), in_hbm(off_diag), in_hbm(diag_block))
+    )(
+        in_hbm(block_of_device),
+        in_hbm(interface_pairs),
+        in_hbm(right_side),
+        in_hbm(off_diag),
+        in_hbm(diag_block),
+    )
 
     lines = count // PLANE
     if lines <= 8:
-        tokens = [token] + [crossed(token, PLANE * k) for k in range(1, lines)]
+        order = LINE_ORDER if lines == 4 else range(1, lines)
+        tokens = [token] + [crossed(token, PLANE * k) for k in order]
     else:
         groups = [[PLANE * k + j for k in range(lines)] for j in range(PLANE)]
         gathered = lax.all_gather(token, "blk", axis_index_groups=groups)
         tokens = [gathered[k] for k in range(lines)]
 
-    inside, edges = pl.pallas_call(
-        interior_kernel,
-        out_shape=(pltpu.HBM(right_side.shape, F32), VMEM((2, 5, 8, 128), F32)),
-        in_specs=[whole, whole, whole],
-        out_specs=(any_space, whole),
-        scratch_shapes=[
+    rows_early = rows // 2 // TILE * TILE
+    factors, first_sweep, upper = pl.pallas_call(
+        early_kernel,
+        out_shape=(
             VMEM((5, 5, rows, 128), F32),
             VMEM((5, rows + 16, 128), F32),
-            VMEM((5, rows + 16, 128), F32),
-            pltpu.SemaphoreType.DMA((1,)),
-        ],
-        compiler_params=pltpu.CompilerParams(vmem_limit_bytes=16 * MIB),
+            VMEM((5, rows_early, 128), F32),
+        ),
+        in_specs=[any_space, whole, whole, whole],
+        out_specs=(whole, whole, whole),
+        scratch_shapes=[VMEM((5, rows + 16, 128), F32)],
+        compiler_params=pltpu.CompilerParams(vmem_limit_bytes=12 * MIB),
         cost_estimate=pl.CostEstimate(
-            flops=32000000, bytes_accessed=12 * MIB, transcendentals=0
-        ),
-        name="interior",
-    )(in_vmem(right_side), in_vmem(off_diag), in_vmem(diag_block))
+            flops=20000000, bytes_accessed=12 * MIB, transcendentals=0
+        ),
+        name="early",
+    )(token, in_vmem(right_side), in_vmem(off_diag), in_vmem(diag_block))
 
     chosen = pl.pallas_call(
         select_kernel,
         out_shape=[VMEM((2 * TOKEN, 128), F32)] * PLANE,
-        in_specs=[whole] * len(tokens),
+        in_specs=[whole] * len(tokens) + [any_space],
         out_specs=[whole] * PLANE,
         compiler_params=pltpu.CompilerParams(vmem_limit_bytes=8 * MIB),
         name="choose",
-    )(*[in_vmem(value) for value in tokens])
-    arrived = [chosen[0]] + [crossed(chosen[k], k) for k in range(1, PLANE)]
+    )(*[in_vmem(value) for value in tokens], upper)
+
+    inside, lower = pl.pallas_call(
+        late_kernel,
+        out_shape=(
+            pltpu.HBM(right_side.shape, F32),
+            VMEM((5, rows - rows_early, 128), F32),
+        ),
+        in_specs=[whole] * 5,
+        out_specs=(any_space, whole),
+        scratch_shapes=[pltpu.SemaphoreType.DMA((2,))],
+        compiler_params=pltpu.CompilerParams(vmem_limit_bytes=8 * MIB),
+        cost_estimate=pl.CostEstimate(
+            flops=8000000, bytes_accessed=6 * MIB, transcendentals=0
+        ),
+        name="late",
+    )(*[in_vmem(value) for value in (right_side, off_diag, factors, first_sweep, upper)])
+    arrived = [chosen[0]] + [crossed(chosen[k], k) for k in PLANE_ORDER]
 
     return pl.pallas_call(
         finish_kernel,
         out_shape=pltpu.HBM(right_side.shape, F32),
-        in_specs=[any_space] + [whole] * (1 + PLANE + 4),
+        in_specs=[any_space] + [whole] * (1 + PLANE + 5),
         out_specs=any_space,
         scratch_shapes=[
             VMEM((2, TOKEN, 128), F32),
@@ -361,7 +436,8 @@
         strip_order,
         in_vmem(off_edge),
         in_vmem(factors_edge),
-        in_vmem(edges),
+        in_vmem(upper),
+        in_vmem(lower),
     )
 
 

time: 23 us -> 17.2 us (0.75)
  waiting for transfers between devices: 4.27 us -> 1.57 us
  local copies, waits for them, and re-layouts: 1.87 us -> 0.01 us
  Pallas kernels: 8.91 us -> 7.82 us
    ppermute x6, waiting for transfers between devices: 4.27 us -> 1.57 us  [crossed(): return lax.ppermute(value, 'blk', [(i, i ^ by) for i in range(count)])]
    unnamed x12 -> x8, local copies, waits for them, and re-layouts: 1.87 us -> 0.01 us
    pallas_call x1, Pallas kernels: 2.77 us -> 1.73 us  [on_device(): pl.pallas_call(edge_kernel, out_shape=(VMEM((2 * TOKEN, 128), F32), VMEM(...]
    pallas_call x1 -> x2, Pallas kernels: 5.16 us -> 5.12 us  [the longest x1 3.46 us: on_device(): pl.pallas_call(early_kernel, out_shape=(VMEM((5, 5, rows, 128), F32), VME...]
  transfers between devices with their start and end apart: 6 -> 6, of which waited for: 2 -> 3; matrix products, arithmetic and copies ran while one was open for 0% -> 0% of each run, Pallas kernels for 23% -> 30%
where the time goes in v2:
time: 17.2 us; the launch traced here: 17.1 us
  Pallas kernels  7.82 us (45%)
  starting transfers between devices  7.61 us (44%)
  waiting for transfers between devices  1.57 us (9%)
    ppermute x6, starting transfers between devices, crossed(): return lax.ppermute(value, 'blk', [(i, i ^ by) for i in range(count)])  7.61 us
    pallas_call x1, Pallas kernels, on_device(): pl.pallas_call(early_kernel, out_shape=(VMEM((5, 5, rows, 128), F32), VME...  3.46 us
    pallas_call x1, Pallas kernels, on_device(): pl.pallas_call(edge_kernel, out_shape=(VMEM((2 * TOKEN, 128), F32), VMEM(...  1.73 us
    pallas_call x1, Pallas kernels, on_device(): pl.pallas_call(late_kernel, out_shape=(pltpu.HBM(right_side.shape, F32),...  1.66 us
    ppermute x6, waiting for transfers between devices, crossed(): return lax.ppermute(value, 'blk', [(i, i ^ by) for i in range(count)])  1.57 us
    pallas_call x1, Pallas kernels, on_device(): pl.pallas_call(finish_kernel, out_shape=pltpu.HBM(right_side.shape, F32),...  0.88 us
  transfers between devices with their start and end apart: 6, of which 3 were waited for; matrix products, arithmetic and copies ran while one was open for 0% of the time, Pallas kernels for 30%

profile of v2, /device:TPU:0, one launch (start us, length us, event | category | flops | bytes accessed | tf_op | source)
XLA Modules:
  0.0 17.1 jit_solution(11756236113281327271)
XLA Ops:
  0.0 0.0 copy-start.2
  0.0 0.0 copy-start
  0.0 0.0 copy-start.1
  0.0 1.7 %edges.1 = (f32[80,128]{1,0:T(8,128)S(1)}, f32[2,25,8,128]{3,2,1,0:T(8,128)S(1)}, bf16[2,4,5,5,16,128]{5,4,3,2,1,0:T(8,128)(2,1)S(1)}) custom-call(s32[16]{0:T(128)} %blocks_h.1, s32[1,2]{1,0:T(1,128)} %pairs_h.1, f32[5,256,128]{2,1,0:T(8,128)} %rhs.3, bf16[4,5,5,256,128]{4,3,2,1,0:T(8,128)(2,1)} %off.3, f32[5,5,256,128]{3,2,1,0:T(8,128)} %diag.1), custom_call_target="tpu_custom_call" | custom-call | tf_op jit(solution)/shard_map/edges/pallas_call | solution.py:339
  1.7 4.1 %collective-permute-start = (f32[80,128]{1,0:T(8,128)S(1)}, f32[80,128]{1,0:T(8,128)S(1)}, u32[]{:S(2)}, u32[]{:S(2)}) collective-permute-start(f32[80,128]{1,0:T(8,128)S(1)} %get-tuple-element.17.token.refs_0_.refs_1_), channel_id=1, source_target_pairs={{0,8},{1,9},{2,10},{3,11},{4,12},{5,13},{6,14},{7,15},{8,0},{9,1},... | collective-permute-start | bytes 122888 | tf_op jit(solution)/shard_map/ppermute | solution.py:331
  5.9 1.3 %collective-permute-start.1 = (f32[80,128]{1,0:T(8,128)S(1)}, f32[80,128]{1,0:T(8,128)S(1)}, u32[]{:S(2)}, u32[]{:S(2)}) collective-permute-start(f32[80,128]{1,0:T(8,128)S(1)} %get-tuple-element.17.token.refs_0_.refs_1_), channel_id=1, source_target_pairs={{0,12},{1,13},{2,14},{3,15},{4,8},{5,9},{6,10},{7,11},{8,4},{9,5},... | collective-permute-start | bytes 122888 | tf_op jit(solution)/shard_map/ppermute | solution.py:331
  7.2 0.2 %collective-permute-start.2 = (f32[80,128]{1,0:T(8,128)S(1)}, f32[80,128]{1,0:T(8,128)S(1)}, u32[]{:S(2)}, u32[]{:S(2)}) collective-permute-start(f32[80,128]{1,0:T(8,128)S(1)} %get-tuple-element.17.token.refs_0_.refs_1_), channel_id=1, source_target_pairs={{0,4},{1,5},{2,6},{3,7},{4,0},{5,1},{6,2},{7,3},{8,12},{9,13},{10,... | collective-permute-start | bytes 122888 | tf_op jit(solution)/shard_map/ppermute | solution.py:331
  7.4 0.0 copy-done.2
  7.4 0.0 copy-done
  7.4 0.0 copy-done.1
  7.4 3.5 %early.1 = (f32[5,5,256,128]{3,2,1,0:T(8,128)S(1)}, f32[5,272,128]{2,1,0:T(8,128)S(1)}, f32[5,128,128]{2,1,0:T(8,128)S(1)}) custom-call(f32[80,128]{1,0:T(8,128)S(1)} %get-tuple-element.17.token.refs_0_.refs_1_, f32[5,256,128]{2,1,0:T(8,128)S(1)} %copy-done.2, bf16[4,5,5,256,128]{4,3,2,1,0:T(8,128)(2,1)S(1)} %copy-done, f32[5,5,256,128]{3,2,1,0:T(8,128)S(1)} %copy-done.1), custom_call_target="tpu_custom_call" | custom-call | flops 20000000 | bytes 12582912 | tf_op jit(solution)/shard_map/early/pallas_call | solution.py:376
  10.9 0.0 collective-permute-done.refs_1_
  10.9 0.7 %collective-permute-done.1.refs_2_ = f32[80,128]{1,0:T(8,128)S(1)} collective-permute-done((f32[80,128]{1,0:T(8,128)S(1)}, f32[80,128]{1,0:T(8,128)S(1)}, u32[]{:S(2)}, u32[]{:S(2)}) %collective-permute-start.1) | collective-permute-done | bytes 40992 | tf_op jit(solution)/shard_map/ppermute | solution.py:331
  11.7 0.0 collective-permute-done.2.refs_3_
  11.7 0.1 choose.1
  11.8 0.1 collective-permute-start.3
  11.8 1.6 %collective-permute-start.4 = (f32[80,128]{1,0:T(8,128)S(1)}, f32[80,128]{1,0:T(8,128)S(1)}, u32[]{:S(2)}, u32[]{:S(2)}) collective-permute-start(f32[80,128]{1,0:T(8,128)S(1)} %get-tuple-element.24), channel_id=1, source_target_pairs={{0,2},{1,3},{2,0},{3,1},{4,6},{5,7},{6,4},{7,5},{8,10},{9,11},{10,... | collective-permute-start | bytes 122888 | tf_op jit(solution)/shard_map/ppermute | solution.py:331
  13.4 0.3 %collective-permute-start.5 = (f32[80,128]{1,0:T(8,128)S(1)}, f32[80,128]{1,0:T(8,128)S(1)}, u32[]{:S(2)}, u32[]{:S(2)}) collective-permute-start(f32[80,128]{1,0:T(8,128)S(1)} %get-tuple-element.25), channel_id=1, source_target_pairs={{0,1},{1,0},{2,3},{3,2},{4,5},{5,4},{6,7},{7,6},{8,9},{9,8},{10,11... | collective-permute-start | bytes 122888 | tf_op jit(solution)/shard_map/ppermute | solution.py:331
  13.7 0.0 copy-start.3
  13.7 1.7 %late.1 = (f32[5,256,128]{2,1,0:T(8,128)}, f32[5,128,128]{2,1,0:T(8,128)S(1)}) custom-call(f32[5,256,128]{2,1,0:T(8,128)S(1)} %copy-done.2, bf16[4,5,5,256,128]{4,3,2,1,0:T(8,128)(2,1)S(1)} %copy-done, f32[5,5,256,128]{3,2,1,0:T(8,128)S(1)} %get-tuple-element.18.factors, f32[5,272,128]{2,1,0:T(8,128)S(1)} %get-tuple-element.19.first_sweep, ...), custom_call_target="tpu_custom_call" | custom-call | flops 8000000 | bytes 6291456 | tf_op jit(solution)/shard_map/late/pallas_call | solution.py:402
  15.4 0.3 %collective-permute-done.3.refs_3_ = f32[80,128]{1,0:T(8,128)S(1)} collective-permute-done((f32[80,128]{1,0:T(8,128)S(1)}, f32[80,128]{1,0:T(8,128)S(1)}, u32[]{:S(2)}, u32[]{:S(2)}) %collective-permute-start.3) | collective-permute-done | bytes 40992 | tf_op jit(solution)/shard_map/ppermute | solution.py:331
  15.6 0.6 %collective-permute-done.4.refs_4_ = f32[80,128]{1,0:T(8,128)S(1)} collective-permute-done((f32[80,128]{1,0:T(8,128)S(1)}, f32[80,128]{1,0:T(8,128)S(1)}, u32[]{:S(2)}, u32[]{:S(2)}) %collective-permute-start.4) | collective-permute-done | bytes 40992 | tf_op jit(solution)/shard_map/ppermute | solution.py:331
  16.2 0.0 collective-permute-done.5.refs_5_
  16.2 0.0 copy-done.3
  16.2 0.9 %finish.1 = f32[5,256,128]{2,1,0:T(8,128)} custom-call(f32[5,256,128]{2,1,0:T(8,128)} %get-tuple-element.21.refs_0_, f32[80,128]{1,0:T(8,128)S(1)} %get-tuple-element.17.token.refs_0_.refs_1_, f32[80,128]{1,0:T(8,128)S(1)} %get-tuple-element.22.refs_2_, f32[80,128]{1,0:T(8,128)S(1)} %collective-permute-done.3.refs_3_, ...), custom_call_target="tpu_custom_call", output_to_operand_aliasing={{}: (0, {})} | custom-call | tf_op jit(solution)/shard_map/finish/pallas_call | solution.py:419
Async XLA Ops:
  0.0 7.4 %copy-start.2 = (f32[5,256,128]{2,1,0:T(8,128)S(1)}, f32[5,256,128]{2,1,0:T(8,128)}, u32[]{:S(2)}) copy-start(f32[5,256,128]{2,1,0:T(8,128)} %rhs.3) | copy-start | bytes 1966084
  0.0 7.4 %copy-start = (bf16[4,5,5,256,128]{4,3,2,1,0:T(8,128)(2,1)S(1)}, bf16[4,5,5,256,128]{4,3,2,1,0:T(8,128)(2,1)}, u32[]{:S(2)}) copy-start(bf16[4,5,5,256,128]{4,3,2,1,0:T(8,128)(2,1)} %off.3) | copy-start | bytes 19660804
  0.0 7.4 %copy-start.1 = (f32[5,5,256,128]{3,2,1,0:T(8,128)S(1)}, f32[5,5,256,128]{3,2,1,0:T(8,128)}, u32[]{:S(2)}) copy-start(f32[5,5,256,128]{3,2,1,0:T(8,128)} %diag.1) | copy-start | bytes 9830404
  1.7 9.2 %collective-permute-start = (f32[80,128]{1,0:T(8,128)S(1)}, f32[80,128]{1,0:T(8,128)S(1)}, u32[]{:S(2)}, u32[]{:S(2)}) collective-permute-start(f32[80,128]{1,0:T(8,128)S(1)} %get-tuple-element.17.token.refs_0_.refs_1_), channel_id=1, source_target_pairs={{0,8},{1,9},{2,10},{3,11},{4,12},{5,13},{6,14},{7,15},{8,0},{9,1},... | collective-permute-start | bytes 122888 | tf_op jit(solution)/shard_map/ppermute | solution.py:331
  5.9 5.8 %collective-permute-start.1 = (f32[80,128]{1,0:T(8,128)S(1)}, f32[80,128]{1,0:T(8,128)S(1)}, u32[]{:S(2)}, u32[]{:S(2)}) collective-permute-start(f32[80,128]{1,0:T(8,128)S(1)} %get-tuple-element.17.token.refs_0_.refs_1_), channel_id=1, source_target_pairs={{0,12},{1,13},{2,14},{3,15},{4,8},{5,9},{6,10},{7,11},{8,4},{9,5},... | collective-permute-start | bytes 122888 | tf_op jit(solution)/shard_map/ppermute | solution.py:331
  7.2 4.5 %collective-permute-start.2 = (f32[80,128]{1,0:T(8,128)S(1)}, f32[80,128]{1,0:T(8,128)S(1)}, u32[]{:S(2)}, u32[]{:S(2)}) collective-permute-start(f32[80,128]{1,0:T(8,128)S(1)} %get-tuple-element.17.token.refs_0_.refs_1_), channel_id=1, source_target_pairs={{0,4},{1,5},{2,6},{3,7},{4,0},{5,1},{6,2},{7,3},{8,12},{9,13},{10,... | collective-permute-start | bytes 122888 | tf_op jit(solution)/shard_map/ppermute | solution.py:331
  11.8 3.9 %collective-permute-start.3 = (f32[80,128]{1,0:T(8,128)S(1)}, f32[80,128]{1,0:T(8,128)S(1)}, u32[]{:S(2)}, u32[]{:S(2)}) collective-permute-start(f32[80,128]{1,0:T(8,128)S(1)} %get-tuple-element.23), channel_id=1, source_target_pairs={{0,3},{1,2},{2,1},{3,0},{4,7},{5,6},{6,5},{7,4},{8,11},{9,10},{10,... | collective-permute-start | bytes 122888 | tf_op jit(solution)/shard_map/ppermute | solution.py:331
  11.8 4.3 %collective-permute-start.4 = (f32[80,128]{1,0:T(8,128)S(1)}, f32[80,128]{1,0:T(8,128)S(1)}, u32[]{:S(2)}, u32[]{:S(2)}) collective-permute-start(f32[80,128]{1,0:T(8,128)S(1)} %get-tuple-element.24), channel_id=1, source_target_pairs={{0,2},{1,3},{2,0},{3,1},{4,6},{5,7},{6,4},{7,5},{8,10},{9,11},{10,... | collective-permute-start | bytes 122888 | tf_op jit(solution)/shard_map/ppermute | solution.py:331
  13.4 2.8 %collective-permute-start.5 = (f32[80,128]{1,0:T(8,128)S(1)}, f32[80,128]{1,0:T(8,128)S(1)}, u32[]{:S(2)}, u32[]{:S(2)}) collective-permute-start(f32[80,128]{1,0:T(8,128)S(1)} %get-tuple-element.25), channel_id=1, source_target_pairs={{0,1},{1,0},{2,3},{3,2},{4,5},{5,4},{6,7},{7,6},{8,9},{9,8},{10,11... | collective-permute-start | bytes 122888 | tf_op jit(solution)/shard_map/ppermute | solution.py:331
  13.7 2.5 %copy-start.3 = (s32[1,2,128]{2,1,0:T(2,128)S(1)}, s32[1,2,128]{2,1,0:T(2,128)}, u32[]{:S(2)}) copy-start(s32[1,2,128]{2,1,0:T(2,128)} %refs_6_.1) | copy-start | bytes 3076

commit v3 on v2

--- a/solution.py
+++ b/solution.py
@@ -14,8 +14,8 @@
 PLANE = 4
 MIB = 2**20
 FACTOR_TILE, TILE = 32, 64
-LINE_ORDER = (2, 3, 1)
-PLANE_ORDER = (3, 2, 1)
+LINE_STEPS = ((2, 3, 1, 0), (3, 2, 0, 1), (1, 0, 3, 2))
+PLANE_STEPS = ((3, 2, 1, 0), (2, 3, 0, 1), (1, 0, 3, 2))
 
 
 def lu(entries):
@@ -237,20 +237,29 @@
         copy.wait()
 
 
+def table(values, at):
+    result = values[0]
+    for k in range(1, len(values)):
+        result = jnp.where(at == k, values[k], result)
+    return result
+
+
 def select_kernel(*refs):
     lines = len(refs) - PLANE - 1
     tokens, outs = refs[:lines], refs[lines + 1 :]
     me = lax.axis_index("blk")
-    for other in range(PLANE):
+    place = me % PLANE
+    for out, step in zip(outs, (tuple(range(PLANE)),) + PLANE_STEPS):
+        target = me - place + table(step, place)
         for slot in range(2):
-            wanted = (2 * (me ^ other) + slot).astype(F32)
+            wanted = (2 * target + slot).astype(F32)
             found = jnp.zeros((TOKEN, 128), F32)
             for token in tokens:
                 for side in range(2):
                     code = token[pl.ds(TOKEN * side + CODE_AT, 1)]
                     value = token[pl.ds(TOKEN * side, TOKEN)]
                     found = jnp.where(code == wanted, value, found)
-            outs[other][pl.ds(TOKEN * slot, TOKEN)] = found
+            out[pl.ds(TOKEN * slot, TOKEN)] = found
 
 
 def finish_kernel(*refs):
@@ -268,8 +277,9 @@
         outer = outer_face(side)
         source = own[pl.ds(at + CODE_AT, 1)].astype(jnp.int32) // 2
         found = arrived[0][pl.ds(at, TOKEN)]
-        for value, other in zip(arrived[1:], PLANE_ORDER):
-            here = lax.rem(source, PLANE) == ((me ^ other) % PLANE)
+        for value, step in zip(arrived[1:], PLANE_STEPS):
+            sender = table([step.index(k) for k in range(PLANE)], me % PLANE)
+            here = lax.rem(source, PLANE) == sender
             found = jnp.where(here, value[pl.ds(at, TOKEN)], found)
         columns = jnp.broadcast_to(order[0, side : side + 1], (TOKEN, 128))
         beyond[side] = jnp.take_along_axis(found, columns, axis=1)
@@ -326,9 +336,15 @@
     return pltpu.with_memory_space_constraint(value, pltpu.HBM)
 
 
-def crossed(value, by):
-    count = lax.axis_size("blk")
-    return lax.ppermute(value, "blk", [(i, i ^ by) for i in range(count)])
+def along_line(value, step):
+    pairs = [(PLANE * k + j, PLANE * to + j) for k, to in enumerate(step) for j in range(PLANE)]
+    return lax.ppermute(value, "blk", pairs)
+
+
+def within_plane(value, step):
+    lines = lax.axis_size("blk") // PLANE
+    pairs = [(PLANE * k + j, PLANE * k + to) for k in range(lines) for j, to in enumerate(step)]
+    return lax.ppermute(value, "blk", pairs)
 
 
 def on_device(right_side, off_diag, diag_block, block_of_device, interface_pairs, strip_order):
@@ -365,14 +381,16 @@
 
     lines = count // PLANE
     if lines <= 8:
-        order = LINE_ORDER if lines == 4 else range(1, lines)
-        tokens = [token] + [crossed(token, PLANE * k) for k in order]
+        steps = [[k ^ by for k in range(lines)] for by in range(1, lines)]
+        if lines == len(LINE_STEPS[0]):
+            steps = LINE_STEPS
+        tokens = [token] + [along_line(token, step) for step in steps]
     else:
         groups = [[PLANE * k + j for k in range(lines)] for j in range(PLANE)]
         gathered = lax.all_gather(token, "blk", axis_index_groups=groups)
         tokens = [gathered[k] for k in range(lines)]
 
-    rows_early = rows // 2 // TILE * TILE
+    rows_early = rows // 4 // TILE * TILE
     factors, first_sweep, upper = pl.pallas_call(
         early_kernel,
         out_shape=(
@@ -414,7 +432,9 @@
         ),
         name="late",
     )(*[in_vmem(value) for value in (right_side, off_diag, factors, first_sweep, upper)])
-    arrived = [chosen[0]] + [crossed(chosen[k], k) for k in PLANE_ORDER]
+    arrived = [chosen[0]]
+    for value, step in zip(chosen[1:], PLANE_STEPS):
+        arrived.append(within_plane(value, step))
 
     return pl.pallas_call(
         finish_kernel,

time: 17.2 us -> 16.8 us (0.977)
  waiting for transfers between devices: 1.57 us -> 1.08 us
    pallas_call x1, Pallas kernels: 1.66 us -> 2.18 us  [on_device(): pl.pallas_call(late_kernel, out_shape=(pltpu.HBM(right_side.shape, F32),...]
    ppermute x6, waiting for transfers between devices: 1.57 us -> 1.08 us  [the longest x3 0.78 us: along_line(): return lax.ppermute(value, 'blk', pairs)]
    pallas_call x1, Pallas kernels: 3.46 us -> 3 us  [on_device(): pl.pallas_call(early_kernel, out_shape=(VMEM((5, 5, rows, 128), F32), VME...]
  transfers between devices with their start and end apart: 6 -> 6, of which waited for: 3 -> 3; matrix products, arithmetic and copies ran while one was open for 0% -> 0% of each run, Pallas kernels for 30% -> 31%
where the time goes in v3:
time: 16.8 us; the launch traced here: 16.6 us
  Pallas kernels  7.88 us (47%)
  starting transfers between devices  7.59 us (45%)
  waiting for transfers between devices  1.08 us (6%)
    ppermute x3, starting transfers between devices, along_line(): return lax.ppermute(value, 'blk', pairs)  5.67 us
    pallas_call x1, Pallas kernels, on_device(): pl.pallas_call(early_kernel, out_shape=(VMEM((5, 5, rows, 128), F32), VME...  3 us
    pallas_call x1, Pallas kernels, on_device(): pl.pallas_call(late_kernel, out_shape=(pltpu.HBM(right_side.shape, F32),...  2.18 us
    ppermute x3, starting transfers between devices, within_plane(): return lax.ppermute(value, 'blk', pairs)  1.92 us
    pallas_call x1, Pallas kernels, on_device(): pl.pallas_call(edge_kernel, out_shape=(VMEM((2 * TOKEN, 128), F32), VMEM(...  1.73 us
    pallas_call x1, Pallas kernels, on_device(): pl.pallas_call(finish_kernel, out_shape=pltpu.HBM(right_side.shape, F32),...  0.88 us
    ppermute x3, waiting for transfers between devices, along_line(): return lax.ppermute(value, 'blk', pairs)  0.78 us
  transfers between devices with their start and end apart: 6, of which 3 were waited for; matrix products, arithmetic and copies ran while one was open for 0% of the time, Pallas kernels for 31%

profile of v3, /device:TPU:0, one launch (start us, length us, event | category | flops | bytes accessed | tf_op | source)
XLA Modules:
  0.0 16.6 jit_solution(14755195419149774105)
XLA Ops:
  0.0 0.0 copy-start.2
  0.0 0.0 copy-start
  0.0 0.0 copy-start.1
  0.0 1.7 %edges.1 = (f32[80,128]{1,0:T(8,128)S(1)}, f32[2,25,8,128]{3,2,1,0:T(8,128)S(1)}, bf16[2,4,5,5,16,128]{5,4,3,2,1,0:T(8,128)(2,1)S(1)}) custom-call(s32[16]{0:T(128)} %blocks_h.1, s32[1,2]{1,0:T(1,128)} %pairs_h.1, f32[5,256,128]{2,1,0:T(8,128)} %rhs.3, bf16[4,5,5,256,128]{4,3,2,1,0:T(8,128)(2,1)} %off.3, f32[5,5,256,128]{3,2,1,0:T(8,128)} %diag.1), custom_call_target="tpu_custom_call" | custom-call | tf_op jit(solution)/shard_map/edges/pallas_call | solution.py:355
  1.7 4.1 %collective-permute-start = (f32[80,128]{1,0:T(8,128)S(1)}, f32[80,128]{1,0:T(8,128)S(1)}, u32[]{:S(2)}, u32[]{:S(2)}) collective-permute-start(f32[80,128]{1,0:T(8,128)S(1)} %get-tuple-element.17.token.refs_0_.refs_1_), channel_id=1, source_target_pairs={{0,8},{1,9},{2,10},{3,11},{4,12},{5,13},{6,14},{7,15},{8,4},{9,5},... | collective-permute-start | bytes 122888 | tf_op jit(solution)/shard_map/ppermute | solution.py:341
  5.8 1.1 %collective-permute-start.1 = (f32[80,128]{1,0:T(8,128)S(1)}, f32[80,128]{1,0:T(8,128)S(1)}, u32[]{:S(2)}, u32[]{:S(2)}) collective-permute-start(f32[80,128]{1,0:T(8,128)S(1)} %get-tuple-element.17.token.refs_0_.refs_1_), channel_id=1, source_target_pairs={{0,12},{1,13},{2,14},{3,15},{4,8},{5,9},{6,10},{7,11},{8,0},{9,1},... | collective-permute-start | bytes 122888 | tf_op jit(solution)/shard_map/ppermute | solution.py:341
  6.9 0.5 %collective-permute-start.2 = (f32[80,128]{1,0:T(8,128)S(1)}, f32[80,128]{1,0:T(8,128)S(1)}, u32[]{:S(2)}, u32[]{:S(2)}) collective-permute-start(f32[80,128]{1,0:T(8,128)S(1)} %get-tuple-element.17.token.refs_0_.refs_1_), channel_id=1, source_target_pairs={{0,4},{1,5},{2,6},{3,7},{4,0},{5,1},{6,2},{7,3},{8,12},{9,13},{10,... | collective-permute-start | bytes 122888 | tf_op jit(solution)/shard_map/ppermute | solution.py:341
  7.4 0.0 copy-done.2
  7.4 0.0 copy-done
  7.4 0.0 copy-done.1
  7.4 3.0 %early.1 = (f32[5,5,256,128]{3,2,1,0:T(8,128)S(1)}, f32[5,272,128]{2,1,0:T(8,128)S(1)}, f32[5,64,128]{2,1,0:T(8,128)S(1)}) custom-call(f32[80,128]{1,0:T(8,128)S(1)} %get-tuple-element.17.token.refs_0_.refs_1_, f32[5,256,128]{2,1,0:T(8,128)S(1)} %copy-done.2, bf16[4,5,5,256,128]{4,3,2,1,0:T(8,128)(2,1)S(1)} %copy-done, f32[5,5,256,128]{3,2,1,0:T(8,128)S(1)} %copy-done.1), custom_call_target="tpu_custom_call" | custom-call | flops 20000000 | bytes 12582912 | tf_op jit(solution)/shard_map/early/pallas_call | solution.py:394
  10.4 0.0 collective-permute-done.refs_1_
  10.4 0.4 %collective-permute-done.1.refs_2_ = f32[80,128]{1,0:T(8,128)S(1)} collective-permute-done((f32[80,128]{1,0:T(8,128)S(1)}, f32[80,128]{1,0:T(8,128)S(1)}, u32[]{:S(2)}, u32[]{:S(2)}) %collective-permute-start.1) | collective-permute-done | bytes 40992 | tf_op jit(solution)/shard_map/ppermute | solution.py:341
  10.8 0.4 %collective-permute-done.2.refs_3_ = f32[80,128]{1,0:T(8,128)S(1)} collective-permute-done((f32[80,128]{1,0:T(8,128)S(1)}, f32[80,128]{1,0:T(8,128)S(1)}, u32[]{:S(2)}, u32[]{:S(2)}) %collective-permute-start.2) | collective-permute-done | bytes 40992 | tf_op jit(solution)/shard_map/ppermute | solution.py:341
  11.2 0.1 choose.1
  11.3 0.1 collective-permute-start.3
  11.4 1.6 %collective-permute-start.4 = (f32[80,128]{1,0:T(8,128)S(1)}, f32[80,128]{1,0:T(8,128)S(1)}, u32[]{:S(2)}, u32[]{:S(2)}) collective-permute-start(f32[80,128]{1,0:T(8,128)S(1)} %get-tuple-element.24), channel_id=1, source_target_pairs={{0,2},{1,3},{2,0},{3,1},{4,6},{5,7},{6,4},{7,5},{8,10},{9,11},{10,... | collective-permute-start | bytes 122888 | tf_op jit(solution)/shard_map/ppermute | solution.py:347
  13.0 0.3 %collective-permute-start.5 = (f32[80,128]{1,0:T(8,128)S(1)}, f32[80,128]{1,0:T(8,128)S(1)}, u32[]{:S(2)}, u32[]{:S(2)}) collective-permute-start(f32[80,128]{1,0:T(8,128)S(1)} %get-tuple-element.25), channel_id=1, source_target_pairs={{0,1},{1,0},{2,3},{3,2},{4,5},{5,4},{6,7},{7,6},{8,9},{9,8},{10,11... | collective-permute-start | bytes 122888 | tf_op jit(solution)/shard_map/ppermute | solution.py:347
  13.2 0.0 copy-start.3
  13.2 2.2 %late.1 = (f32[5,256,128]{2,1,0:T(8,128)}, f32[5,192,128]{2,1,0:T(8,128)S(1)}) custom-call(f32[5,256,128]{2,1,0:T(8,128)S(1)} %copy-done.2, bf16[4,5,5,256,128]{4,3,2,1,0:T(8,128)(2,1)S(1)} %copy-done, f32[5,5,256,128]{3,2,1,0:T(8,128)S(1)} %get-tuple-element.18.factors, f32[5,272,128]{2,1,0:T(8,128)S(1)} %get-tuple-element.19.first_sweep, ...), custom_call_target="tpu_custom_call" | custom-call | flops 8000000 | bytes 6291456 | tf_op jit(solution)/shard_map/late/pallas_call | solution.py:420
  15.4 0.0 collective-permute-done.3.refs_3_
  15.4 0.3 %collective-permute-done.4.refs_4_ = f32[80,128]{1,0:T(8,128)S(1)} collective-permute-done((f32[80,128]{1,0:T(8,128)S(1)}, f32[80,128]{1,0:T(8,128)S(1)}, u32[]{:S(2)}, u32[]{:S(2)}) %collective-permute-start.4) | collective-permute-done | bytes 40992 | tf_op jit(solution)/shard_map/ppermute | solution.py:347
  15.7 0.0 collective-permute-done.5.refs_5_
  15.7 0.0 copy-done.3
  15.7 0.9 %finish.1 = f32[5,256,128]{2,1,0:T(8,128)} custom-call(f32[5,256,128]{2,1,0:T(8,128)} %get-tuple-element.21.refs_0_, f32[80,128]{1,0:T(8,128)S(1)} %get-tuple-element.17.token.refs_0_.refs_1_, f32[80,128]{1,0:T(8,128)S(1)} %get-tuple-element.22.refs_2_, f32[80,128]{1,0:T(8,128)S(1)} %collective-permute-done.3.refs_3_, ...), custom_call_target="tpu_custom_call", output_to_operand_aliasing={{}: (0, {})} | custom-call | tf_op jit(solution)/shard_map/finish/pallas_call | solution.py:439
Async XLA Ops:
  0.0 7.4 %copy-start.2 = (f32[5,256,128]{2,1,0:T(8,128)S(1)}, f32[5,256,128]{2,1,0:T(8,128)}, u32[]{:S(2)}) copy-start(f32[5,256,128]{2,1,0:T(8,128)} %rhs.3) | copy-start | bytes 1966084
  0.0 7.4 %copy-start = (bf16[4,5,5,256,128]{4,3,2,1,0:T(8,128)(2,1)S(1)}, bf16[4,5,5,256,128]{4,3,2,1,0:T(8,128)(2,1)}, u32[]{:S(2)}) copy-start(bf16[4,5,5,256,128]{4,3,2,1,0:T(8,128)(2,1)} %off.3) | copy-start | bytes 19660804
  0.0 7.4 %copy-start.1 = (f32[5,5,256,128]{3,2,1,0:T(8,128)S(1)}, f32[5,5,256,128]{3,2,1,0:T(8,128)}, u32[]{:S(2)}) copy-start(f32[5,5,256,128]{3,2,1,0:T(8,128)} %diag.1) | copy-start | bytes 9830404
  1.7 8.7 %collective-permute-start = (f32[80,128]{1,0:T(8,128)S(1)}, f32[80,128]{1,0:T(8,128)S(1)}, u32[]{:S(2)}, u32[]{:S(2)}) collective-permute-start(f32[80,128]{1,0:T(8,128)S(1)} %get-tuple-element.17.token.refs_0_.refs_1_), channel_id=1, source_target_pairs={{0,8},{1,9},{2,10},{3,11},{4,12},{5,13},{6,14},{7,15},{8,4},{9,5},... | collective-permute-start | bytes 122888 | tf_op jit(solution)/shard_map/ppermute | solution.py:341
  5.8 5.0 %collective-permute-start.1 = (f32[80,128]{1,0:T(8,128)S(1)}, f32[80,128]{1,0:T(8,128)S(1)}, u32[]{:S(2)}, u32[]{:S(2)}) collective-permute-start(f32[80,128]{1,0:T(8,128)S(1)} %get-tuple-element.17.token.refs_0_.refs_1_), channel_id=1, source_target_pairs={{0,12},{1,13},{2,14},{3,15},{4,8},{5,9},{6,10},{7,11},{8,0},{9,1},... | collective-permute-start | bytes 122888 | tf_op jit(solution)/shard_map/ppermute | solution.py:341
  6.9 4.3 %collective-permute-start.2 = (f32[80,128]{1,0:T(8,128)S(1)}, f32[80,128]{1,0:T(8,128)S(1)}, u32[]{:S(2)}, u32[]{:S(2)}) collective-permute-start(f32[80,128]{1,0:T(8,128)S(1)} %get-tuple-element.17.token.refs_0_.refs_1_), channel_id=1, source_target_pairs={{0,4},{1,5},{2,6},{3,7},{4,0},{5,1},{6,2},{7,3},{8,12},{9,13},{10,... | collective-permute-start | bytes 122888 | tf_op jit(solution)/shard_map/ppermute | solution.py:341
  11.3 4.1 %collective-permute-start.3 = (f32[80,128]{1,0:T(8,128)S(1)}, f32[80,128]{1,0:T(8,128)S(1)}, u32[]{:S(2)}, u32[]{:S(2)}) collective-permute-start(f32[80,128]{1,0:T(8,128)S(1)} %get-tuple-element.23), channel_id=1, source_target_pairs={{0,3},{1,2},{2,1},{3,0},{4,7},{5,6},{6,5},{7,4},{8,11},{9,10},{10,... | collective-permute-start | bytes 122888 | tf_op jit(solution)/shard_map/ppermute | solution.py:347
  11.4 4.3 %collective-permute-start.4 = (f32[80,128]{1,0:T(8,128)S(1)}, f32[80,128]{1,0:T(8,128)S(1)}, u32[]{:S(2)}, u32[]{:S(2)}) collective-permute-start(f32[80,128]{1,0:T(8,128)S(1)} %get-tuple-element.24), channel_id=1, source_target_pairs={{0,2},{1,3},{2,0},{3,1},{4,6},{5,7},{6,4},{7,5},{8,10},{9,11},{10,... | collective-permute-start | bytes 122888 | tf_op jit(solution)/shard_map/ppermute | solution.py:347
  13.0 2.8 %collective-permute-start.5 = (f32[80,128]{1,0:T(8,128)S(1)}, f32[80,128]{1,0:T(8,128)S(1)}, u32[]{:S(2)}, u32[]{:S(2)}) collective-permute-start(f32[80,128]{1,0:T(8,128)S(1)} %get-tuple-element.25), channel_id=1, source_target_pairs={{0,1},{1,0},{2,3},{3,2},{4,5},{5,4},{6,7},{7,6},{8,9},{9,8},{10,11... | collective-permute-start | bytes 122888 | tf_op jit(solution)/shard_map/ppermute | solution.py:347
  13.2 2.5 %copy-start.3 = (s32[1,2,128]{2,1,0:T(2,128)S(1)}, s32[1,2,128]{2,1,0:T(2,128)}, u32[]{:S(2)}) copy-start(s32[1,2,128]{2,1,0:T(2,128)} %refs_6_.1) | copy-start | bytes 3076

commit v4 on v3

--- a/solution.py
+++ b/solution.py
@@ -9,7 +9,7 @@
 
 F32 = jnp.float32
 VMEM = pltpu.VMEM
-TOKEN = 40
+TOKEN = 36
 A_AT, M_AT, CODE_AT = 5, 10, 35
 PLANE = 4
 MIB = 2**20
@@ -103,6 +103,22 @@
             copies[side][part].start()
     for copy in scalars:
         copy.start()
+    lane = lax.broadcasted_iota(jnp.int32, (8, 128), 1)
+    lus, rhss, u0s = [], [], []
+    for side in range(2):
+        copies[side][0].wait()
+        copies[side][1].wait()
+        e = lu([[diag_edge[side, a, b] for b in range(5)] for a in range(5)])
+        rhs = [rhs_edge[side, a] for a in range(5)]
+        u0 = solve(lambda a, b: e[a][b], rhs)
+        lus.append(e)
+        rhss.append(rhs)
+        u0s.append(u0)
+        edge_row = 0 if side == 0 else 7
+        for a in range(5):
+            token[pl.ds(TOKEN * side + a, 1)] = u0[a][edge_row : edge_row + 1]
+            for b in range(5):
+                factors[side, 5 * a + b] = e[a][b]
     for copy in scalars:
         copy.wait()
     count = blocks.shape[0]
@@ -115,11 +131,12 @@
         jnp.where(first_end, jnp.maximum(pairs[0, 0], 0), 2 * before + 1),
         jnp.where(last_end, jnp.maximum(pairs[0, 1], 0), 2 * after),
     )
-    lane = lax.broadcasted_iota(jnp.int32, (8, 128), 1)
     for side in range(2):
-        for part in range(3):
-            copies[side][part].wait()
+        token[pl.ds(TOKEN * side + CODE_AT, 1)] = jnp.full(
+            (1, 128), codes[side], jnp.int32
+        ).astype(F32)
     for side in range(2):
+        copies[side][2].wait()
         edge_row = 0 if side == 0 else 7
         half = slice(0, 8) if side == 0 else slice(8, 16)
         outer, inner = (0, 1) if side == 0 else (1, 0)
@@ -127,14 +144,9 @@
         def off(face, a, b):
             return off_edge[side, face, a, b].astype(F32)[half]
 
-        e = lu([[diag_edge[side, a, b] for b in range(5)] for a in range(5)])
-        for a in range(5):
-            for b in range(5):
-                factors[side, 5 * a + b] = e[a][b]
+        e, u0 = lus[side], u0s[side]
         factor_at = lambda a, b: e[a][b]
-        rhs = [rhs_edge[side, a] for a in range(5)]
-        u0 = solve(factor_at, rhs)
-        acc = list(rhs)
+        acc = list(rhss[side])
         for b in range(5):
             around = (
                 (inner, pltpu.roll(u0[b], 7 if side == 0 else 1, 0)),
@@ -147,16 +159,11 @@
         base = solve(factor_at, acc)
         at = TOKEN * side
         for a in range(5):
-            token[pl.ds(at + a, 1)] = u0[a][edge_row : edge_row + 1]
             token[pl.ds(at + A_AT + a, 1)] = base[a][edge_row : edge_row + 1]
         for b in range(5):
             column = solve(factor_at, [off(outer, a, b) for a in range(5)])
             for a in range(5):
                 token[pl.ds(at + M_AT + 5 * a + b, 1)] = column[a][edge_row : edge_row + 1]
-        token[pl.ds(at + CODE_AT, 1)] = jnp.full((1, 128), codes[side], jnp.int32).astype(F32)
-        token[pl.ds(at + CODE_AT + 1, TOKEN - CODE_AT - 1)] = jnp.zeros(
-            (TOKEN - CODE_AT - 1, 128), F32
-        )
 
 
 def sweep_rows(source, rhs, off, factors, at, tile):
@@ -281,8 +288,10 @@
             sender = table([step.index(k) for k in range(PLANE)], me % PLANE)
             here = lax.rem(source, PLANE) == sender
             found = jnp.where(here, value[pl.ds(at, TOKEN)], found)
-        columns = jnp.broadcast_to(order[0, side : side + 1], (TOKEN, 128))
-        beyond[side] = jnp.take_along_axis(found, columns, axis=1)
+        columns = jnp.broadcast_to(order[0, side : side + 1], (8, 128))
+        for first in (0, 8, 16, 24, TOKEN - 8):
+            rows8 = found[first : first + 8]
+            beyond[side, pl.ds(first, 8)] = jnp.take_along_axis(rows8, columns, axis=1)
 
         def mine(k):
             return own[pl.ds(at + k, 1)]
@@ -442,7 +451,7 @@
         in_specs=[any_space] + [whole] * (1 + PLANE + 5),
         out_specs=any_space,
         scratch_shapes=[
-            VMEM((2, TOKEN, 128), F32),
+            VMEM((2, TOKEN + 4, 128), F32),
             VMEM((2, 5, 8, 128), F32),
             pltpu.SemaphoreType.DMA((2,)),
         ],

time: 16.8 us -> 16.4 us (0.976)
  waiting for transfers between devices: 1.08 us -> 0.41 us
  Pallas kernels: 7.88 us -> 8.13 us
    ppermute x3, waiting for transfers between devices: 0.78 us -> 0.41 us  [along_line(): return lax.ppermute(value, 'blk', pairs)]
    ppermute x3, waiting for transfers between devices: 0.3 us -> 0.01 us  [within_plane(): return lax.ppermute(value, 'blk', pairs)]
    pallas_call x1, Pallas kernels: 3 us -> 3.25 us  [on_device(): pl.pallas_call(early_kernel, out_shape=(VMEM((5, 5, rows, 128), F32), VME...]
  transfers between devices with their start and end apart: 6 -> 6, of which waited for: 3 -> 1; matrix products, arithmetic and copies ran while one was open for 0% -> 0% of each run, Pallas kernels for 31% -> 34%
where the time goes in v4:
time: 16.4 us; the launch traced here: 16.2 us
  Pallas kernels  8.13 us (50%)
  starting transfers between devices  7.6 us (46%)
  waiting for transfers between devices  0.41 us (2%)
    ppermute x3, starting transfers between devices, along_line(): return lax.ppermute(value, 'blk', pairs)  5.67 us
    pallas_call x1, Pallas kernels, on_device(): pl.pallas_call(early_kernel, out_shape=(VMEM((5, 5, rows, 128), F32), VME...  3.25 us
    pallas_call x1, Pallas kernels, on_device(): pl.pallas_call(late_kernel, out_shape=(pltpu.HBM(right_side.shape, F32),...  2.29 us
    ppermute x3, starting transfers between devices, within_plane(): return lax.ppermute(value, 'blk', pairs)  1.93 us
    pallas_call x1, Pallas kernels, on_device(): pl.pallas_call(edge_kernel, out_shape=(VMEM((2 * TOKEN, 128), F32), VMEM(...  1.6 us
    pallas_call x1, Pallas kernels, on_device(): pl.pallas_call(finish_kernel, out_shape=pltpu.HBM(right_side.shape, F32),...  0.89 us
    ppermute x3, waiting for transfers between devices, along_line(): return lax.ppermute(value, 'blk', pairs)  0.41 us
  transfers between devices with their start and end apart: 6, of which 1 were waited for; matrix products, arithmetic and copies ran while one was open for 0% of the time, Pallas kernels for 34%

profile of v4, /device:TPU:0, one launch (start us, length us, event | category | flops | bytes accessed | tf_op | source)
XLA Modules:
  0.0 16.2 jit_solution(3109118094794345110)
XLA Ops:
  0.0 0.0 copy-start.2
  0.0 0.0 copy-start
  0.0 0.0 copy-start.1
  0.0 1.6 %edges.1 = (f32[72,128]{1,0:T(8,128)S(1)}, f32[2,25,8,128]{3,2,1,0:T(8,128)S(1)}, bf16[2,4,5,5,16,128]{5,4,3,2,1,0:T(8,128)(2,1)S(1)}) custom-call(s32[16]{0:T(128)} %blocks_h.1, s32[1,2]{1,0:T(1,128)} %pairs_h.1, f32[5,256,128]{2,1,0:T(8,128)} %rhs.3, bf16[4,5,5,256,128]{4,3,2,1,0:T(8,128)(2,1)} %off.3, f32[5,5,256,128]{3,2,1,0:T(8,128)} %diag.1), custom_call_target="tpu_custom_call" | custom-call | tf_op jit(solution)/shard_map/edges/pallas_call | solution.py:364
  1.6 4.1 %collective-permute-start = (f32[72,128]{1,0:T(8,128)S(1)}, f32[72,128]{1,0:T(8,128)S(1)}, u32[]{:S(2)}, u32[]{:S(2)}) collective-permute-start(f32[72,128]{1,0:T(8,128)S(1)} %get-tuple-element.17.token.refs_0_.refs_1_), channel_id=1, source_target_pairs={{0,8},{1,9},{2,10},{3,11},{4,12},{5,13},{6,14},{7,15},{8,4},{9,5},... | collective-permute-start | bytes 110600 | tf_op jit(solution)/shard_map/ppermute | solution.py:350
  5.7 1.1 %collective-permute-start.1 = (f32[72,128]{1,0:T(8,128)S(1)}, f32[72,128]{1,0:T(8,128)S(1)}, u32[]{:S(2)}, u32[]{:S(2)}) collective-permute-start(f32[72,128]{1,0:T(8,128)S(1)} %get-tuple-element.17.token.refs_0_.refs_1_), channel_id=1, source_target_pairs={{0,12},{1,13},{2,14},{3,15},{4,8},{5,9},{6,10},{7,11},{8,0},{9,1},... | collective-permute-start | bytes 110600 | tf_op jit(solution)/shard_map/ppermute | solution.py:350
  6.8 0.5 %collective-permute-start.2 = (f32[72,128]{1,0:T(8,128)S(1)}, f32[72,128]{1,0:T(8,128)S(1)}, u32[]{:S(2)}, u32[]{:S(2)}) collective-permute-start(f32[72,128]{1,0:T(8,128)S(1)} %get-tuple-element.17.token.refs_0_.refs_1_), channel_id=1, source_target_pairs={{0,4},{1,5},{2,6},{3,7},{4,0},{5,1},{6,2},{7,3},{8,12},{9,13},{10,... | collective-permute-start | bytes 110600 | tf_op jit(solution)/shard_map/ppermute | solution.py:350
  7.3 0.0 copy-done.2
  7.3 0.0 copy-done
  7.3 0.0 copy-done.1
  7.3 3.2 %early.1 = (f32[5,5,256,128]{3,2,1,0:T(8,128)S(1)}, f32[5,272,128]{2,1,0:T(8,128)S(1)}, f32[5,64,128]{2,1,0:T(8,128)S(1)}) custom-call(f32[72,128]{1,0:T(8,128)S(1)} %get-tuple-element.17.token.refs_0_.refs_1_, f32[5,256,128]{2,1,0:T(8,128)S(1)} %copy-done.2, bf16[4,5,5,256,128]{4,3,2,1,0:T(8,128)(2,1)S(1)} %copy-done, f32[5,5,256,128]{3,2,1,0:T(8,128)S(1)} %copy-done.1), custom_call_target="tpu_custom_call" | custom-call | flops 20000000 | bytes 12582912 | tf_op jit(solution)/shard_map/early/pallas_call | solution.py:403
  10.5 0.0 collective-permute-done.refs_1_
  10.6 0.0 collective-permute-done.1.refs_2_
  10.6 0.4 %collective-permute-done.2.refs_3_ = f32[72,128]{1,0:T(8,128)S(1)} collective-permute-done((f32[72,128]{1,0:T(8,128)S(1)}, f32[72,128]{1,0:T(8,128)S(1)}, u32[]{:S(2)}, u32[]{:S(2)}) %collective-permute-start.2) | collective-permute-done | bytes 36896 | tf_op jit(solution)/shard_map/ppermute | solution.py:350
  11.0 0.1 choose.1
  11.1 0.1 collective-permute-start.3
  11.1 1.6 %collective-permute-start.4 = (f32[72,128]{1,0:T(8,128)S(1)}, f32[72,128]{1,0:T(8,128)S(1)}, u32[]{:S(2)}, u32[]{:S(2)}) collective-permute-start(f32[72,128]{1,0:T(8,128)S(1)} %get-tuple-element.24), channel_id=1, source_target_pairs={{0,2},{1,3},{2,0},{3,1},{4,6},{5,7},{6,4},{7,5},{8,10},{9,11},{10,... | collective-permute-start | bytes 110600 | tf_op jit(solution)/shard_map/ppermute | solution.py:356
  12.7 0.3 %collective-permute-start.5 = (f32[72,128]{1,0:T(8,128)S(1)}, f32[72,128]{1,0:T(8,128)S(1)}, u32[]{:S(2)}, u32[]{:S(2)}) collective-permute-start(f32[72,128]{1,0:T(8,128)S(1)} %get-tuple-element.25), channel_id=1, source_target_pairs={{0,1},{1,0},{2,3},{3,2},{4,5},{5,4},{6,7},{7,6},{8,9},{9,8},{10,11... | collective-permute-start | bytes 110600 | tf_op jit(solution)/shard_map/ppermute | solution.py:356
  13.0 0.0 copy-start.3
  13.0 2.3 %late.1 = (f32[5,256,128]{2,1,0:T(8,128)}, f32[5,192,128]{2,1,0:T(8,128)S(1)}) custom-call(f32[5,256,128]{2,1,0:T(8,128)S(1)} %copy-done.2, bf16[4,5,5,256,128]{4,3,2,1,0:T(8,128)(2,1)S(1)} %copy-done, f32[5,5,256,128]{3,2,1,0:T(8,128)S(1)} %get-tuple-element.18.factors, f32[5,272,128]{2,1,0:T(8,128)S(1)} %get-tuple-element.19.first_sweep, ...), custom_call_target="tpu_custom_call" | custom-call | flops 8000000 | bytes 6291456 | tf_op jit(solution)/shard_map/late/pallas_call | solution.py:429
  15.3 0.0 collective-permute-done.3.refs_3_
  15.3 0.0 collective-permute-done.4.refs_4_
  15.3 0.0 collective-permute-done.5.refs_5_
  15.3 0.0 copy-done.3
  15.3 0.9 %finish.1 = f32[5,256,128]{2,1,0:T(8,128)} custom-call(f32[5,256,128]{2,1,0:T(8,128)} %get-tuple-element.21.refs_0_, f32[72,128]{1,0:T(8,128)S(1)} %get-tuple-element.17.token.refs_0_.refs_1_, f32[72,128]{1,0:T(8,128)S(1)} %get-tuple-element.22.refs_2_, f32[72,128]{1,0:T(8,128)S(1)} %collective-permute-done.3.refs_3_, ...), custom_call_target="tpu_custom_call", output_to_operand_aliasing={{}: (0, {})} | custom-call | tf_op jit(solution)/shard_map/finish/pallas_call | solution.py:448
Async XLA Ops:
  0.0 7.3 %copy-start.2 = (f32[5,256,128]{2,1,0:T(8,128)S(1)}, f32[5,256,128]{2,1,0:T(8,128)}, u32[]{:S(2)}) copy-start(f32[5,256,128]{2,1,0:T(8,128)} %rhs.3) | copy-start | bytes 1966084
  0.0 7.3 %copy-start = (bf16[4,5,5,256,128]{4,3,2,1,0:T(8,128)(2,1)S(1)}, bf16[4,5,5,256,128]{4,3,2,1,0:T(8,128)(2,1)}, u32[]{:S(2)}) copy-start(bf16[4,5,5,256,128]{4,3,2,1,0:T(8,128)(2,1)} %off.3) | copy-start | bytes 19660804
  0.0 7.3 %copy-start.1 = (f32[5,5,256,128]{3,2,1,0:T(8,128)S(1)}, f32[5,5,256,128]{3,2,1,0:T(8,128)}, u32[]{:S(2)}) copy-start(f32[5,5,256,128]{3,2,1,0:T(8,128)} %diag.1) | copy-start | bytes 9830404
  1.6 8.9 %collective-permute-start = (f32[72,128]{1,0:T(8,128)S(1)}, f32[72,128]{1,0:T(8,128)S(1)}, u32[]{:S(2)}, u32[]{:S(2)}) collective-permute-start(f32[72,128]{1,0:T(8,128)S(1)} %get-tuple-element.17.token.refs_0_.refs_1_), channel_id=1, source_target_pairs={{0,8},{1,9},{2,10},{3,11},{4,12},{5,13},{6,14},{7,15},{8,4},{9,5},... | collective-permute-start | bytes 110600 | tf_op jit(solution)/shard_map/ppermute | solution.py:350
  5.7 4.9 %collective-permute-start.1 = (f32[72,128]{1,0:T(8,128)S(1)}, f32[72,128]{1,0:T(8,128)S(1)}, u32[]{:S(2)}, u32[]{:S(2)}) collective-permute-start(f32[72,128]{1,0:T(8,128)S(1)} %get-tuple-element.17.token.refs_0_.refs_1_), channel_id=1, source_target_pairs={{0,12},{1,13},{2,14},{3,15},{4,8},{5,9},{6,10},{7,11},{8,0},{9,1},... | collective-permute-start | bytes 110600 | tf_op jit(solution)/shard_map/ppermute | solution.py:350
  6.8 4.2 %collective-permute-start.2 = (f32[72,128]{1,0:T(8,128)S(1)}, f32[72,128]{1,0:T(8,128)S(1)}, u32[]{:S(2)}, u32[]{:S(2)}) collective-permute-start(f32[72,128]{1,0:T(8,128)S(1)} %get-tuple-element.17.token.refs_0_.refs_1_), channel_id=1, source_target_pairs={{0,4},{1,5},{2,6},{3,7},{4,0},{5,1},{6,2},{7,3},{8,12},{9,13},{10,... | collective-permute-start | bytes 110600 | tf_op jit(solution)/shard_map/ppermute | solution.py:350
  11.1 4.2 %collective-permute-start.3 = (f32[72,128]{1,0:T(8,128)S(1)}, f32[72,128]{1,0:T(8,128)S(1)}, u32[]{:S(2)}, u32[]{:S(2)}) collective-permute-start(f32[72,128]{1,0:T(8,128)S(1)} %get-tuple-element.23), channel_id=1, source_target_pairs={{0,3},{1,2},{2,1},{3,0},{4,7},{5,6},{6,5},{7,4},{8,11},{9,10},{10,... | collective-permute-start | bytes 110600 | tf_op jit(solution)/shard_map/ppermute | solution.py:356
  11.1 4.2 %collective-permute-start.4 = (f32[72,128]{1,0:T(8,128)S(1)}, f32[72,128]{1,0:T(8,128)S(1)}, u32[]{:S(2)}, u32[]{:S(2)}) collective-permute-start(f32[72,128]{1,0:T(8,128)S(1)} %get-tuple-element.24), channel_id=1, source_target_pairs={{0,2},{1,3},{2,0},{3,1},{4,6},{5,7},{6,4},{7,5},{8,10},{9,11},{10,... | collective-permute-start | bytes 110600 | tf_op jit(solution)/shard_map/ppermute | solution.py:356
  12.7 2.6 %collective-permute-start.5 = (f32[72,128]{1,0:T(8,128)S(1)}, f32[72,128]{1,0:T(8,128)S(1)}, u32[]{:S(2)}, u32[]{:S(2)}) collective-permute-start(f32[72,128]{1,0:T(8,128)S(1)} %get-tuple-element.25), channel_id=1, source_target_pairs={{0,1},{1,0},{2,3},{3,2},{4,5},{5,4},{6,7},{7,6},{8,9},{9,8},{10,11... | collective-permute-start | bytes 110600 | tf_op jit(solution)/shard_map/ppermute | solution.py:356
  13.0 2.3 %copy-start.3 = (s32[1,2,128]{2,1,0:T(2,128)S(1)}, s32[1,2,128]{2,1,0:T(2,128)}, u32[]{:S(2)}) copy-start(s32[1,2,128]{2,1,0:T(2,128)} %refs_6_.1) | copy-start | bytes 3076

commit v5 on v4

--- a/solution.py
+++ b/solution.py
@@ -9,7 +9,7 @@
 
 F32 = jnp.float32
 VMEM = pltpu.VMEM
-TOKEN = 36
+TOKEN = 40
 A_AT, M_AT, CODE_AT = 5, 10, 35
 PLANE = 4
 MIB = 2**20
@@ -119,6 +119,9 @@
             token[pl.ds(TOKEN * side + a, 1)] = u0[a][edge_row : edge_row + 1]
             for b in range(5):
                 factors[side, 5 * a + b] = e[a][b]
+        token[pl.ds(TOKEN * side + CODE_AT + 1, TOKEN - CODE_AT - 1)] = jnp.zeros(
+            (TOKEN - CODE_AT - 1, 128), F32
+        )
     for copy in scalars:
         copy.wait()
     count = blocks.shape[0]
@@ -288,10 +291,8 @@
             sender = table([step.index(k) for k in range(PLANE)], me % PLANE)
             here = lax.rem(source, PLANE) == sender
             found = jnp.where(here, value[pl.ds(at, TOKEN)], found)
-        columns = jnp.broadcast_to(order[0, side : side + 1], (8, 128))
-        for first in (0, 8, 16, 24, TOKEN - 8):
-            rows8 = found[first : first + 8]
-            beyond[side, pl.ds(first, 8)] = jnp.take_along_axis(rows8, columns, axis=1)
+        columns = jnp.broadcast_to(order[0, side : side + 1], (TOKEN, 128))
+        beyond[side] = jnp.take_along_axis(found, columns, axis=1)
 
         def mine(k):
             return own[pl.ds(at + k, 1)]
@@ -451,7 +452,7 @@
         in_specs=[any_space] + [whole] * (1 + PLANE + 5),
         out_specs=any_space,
         scratch_shapes=[
-            VMEM((2, TOKEN + 4, 128), F32),
+            VMEM((2, TOKEN, 128), F32),
             VMEM((2, 5, 8, 128), F32),
             pltpu.SemaphoreType.DMA((2,)),
         ],

time: 16.4 us -> 16.6 us (1.012)
  waiting for transfers between devices: 0.41 us -> 1.08 us
  Pallas kernels: 8.13 us -> 7.75 us
    ppermute x3, waiting for transfers between devices: 0.41 us -> 0.78 us  [along_line(): return lax.ppermute(value, 'blk', pairs)]
    ppermute x3, waiting for transfers between devices: 0.01 us -> 0.3 us  [within_plane(): return lax.ppermute(value, 'blk', pairs)]
    pallas_call x1, Pallas kernels: 3.25 us -> 3 us  [on_device(): pl.pallas_call(early_kernel, out_shape=(VMEM((5, 5, rows, 128), F32), VME...]
  transfers between devices with their start and end apart: 6 -> 6, of which waited for: 1 -> 3; matrix products, arithmetic and copies ran while one was open for 0% -> 0% of each run, Pallas kernels for 34% -> 31%
where the time goes in v5:
time: 16.6 us; the launch traced here: 16.5 us
  Pallas kernels  7.75 us (47%)
  starting transfers between devices  7.59 us (46%)
  waiting for transfers between devices  1.08 us (7%)
    ppermute x3, starting transfers between devices, along_line(): return lax.ppermute(value, 'blk', pairs)  5.67 us
    pallas_call x1, Pallas kernels, on_device(): pl.pallas_call(early_kernel, out_shape=(VMEM((5, 5, rows, 128), F32), VME...  3 us
    pallas_call x1, Pallas kernels, on_device(): pl.pallas_call(late_kernel, out_shape=(pltpu.HBM(right_side.shape, F32),...  2.18 us
    ppermute x3, starting transfers between devices, within_plane(): return lax.ppermute(value, 'blk', pairs)  1.92 us
    pallas_call x1, Pallas kernels, on_device(): pl.pallas_call(edge_kernel, out_shape=(VMEM((2 * TOKEN, 128), F32), VMEM(...  1.6 us
    pallas_call x1, Pallas kernels, on_device(): pl.pallas_call(finish_kernel, out_shape=pltpu.HBM(right_side.shape, F32),...  0.88 us
    ppermute x3, waiting for transfers between devices, along_line(): return lax.ppermute(value, 'blk', pairs)  0.78 us
  transfers between devices with their start and end apart: 6, of which 3 were waited for; matrix products, arithmetic and copies ran while one was open for 0% of the time, Pallas kernels for 31%

profile of v5, /device:TPU:0, one launch (start us, length us, event | category | flops | bytes accessed | tf_op | source)
XLA Modules:
  0.0 16.5 jit_solution(17852916259041974182)
XLA Ops:
  0.0 0.0 copy-start.2
  0.0 0.0 copy-start
  0.0 0.0 copy-start.1
  0.0 1.6 %edges.1 = (f32[80,128]{1,0:T(8,128)S(1)}, f32[2,25,8,128]{3,2,1,0:T(8,128)S(1)}, bf16[2,4,5,5,16,128]{5,4,3,2,1,0:T(8,128)(2,1)S(1)}) custom-call(s32[16]{0:T(128)} %blocks_h.1, s32[1,2]{1,0:T(1,128)} %pairs_h.1, f32[5,256,128]{2,1,0:T(8,128)} %rhs.3, bf16[4,5,5,256,128]{4,3,2,1,0:T(8,128)(2,1)} %off.3, f32[5,5,256,128]{3,2,1,0:T(8,128)} %diag.1), custom_call_target="tpu_custom_call" | custom-call | tf_op jit(solution)/shard_map/edges/pallas_call | solution.py:365
  1.6 4.1 %collective-permute-start = (f32[80,128]{1,0:T(8,128)S(1)}, f32[80,128]{1,0:T(8,128)S(1)}, u32[]{:S(2)}, u32[]{:S(2)}) collective-permute-start(f32[80,128]{1,0:T(8,128)S(1)} %get-tuple-element.17.token.refs_0_.refs_1_), channel_id=1, source_target_pairs={{0,8},{1,9},{2,10},{3,11},{4,12},{5,13},{6,14},{7,15},{8,4},{9,5},... | collective-permute-start | bytes 122888 | tf_op jit(solution)/shard_map/ppermute | solution.py:351
  5.7 1.1 %collective-permute-start.1 = (f32[80,128]{1,0:T(8,128)S(1)}, f32[80,128]{1,0:T(8,128)S(1)}, u32[]{:S(2)}, u32[]{:S(2)}) collective-permute-start(f32[80,128]{1,0:T(8,128)S(1)} %get-tuple-element.17.token.refs_0_.refs_1_), channel_id=1, source_target_pairs={{0,12},{1,13},{2,14},{3,15},{4,8},{5,9},{6,10},{7,11},{8,0},{9,1},... | collective-permute-start | bytes 122888 | tf_op jit(solution)/shard_map/ppermute | solution.py:351
  6.8 0.5 %collective-permute-start.2 = (f32[80,128]{1,0:T(8,128)S(1)}, f32[80,128]{1,0:T(8,128)S(1)}, u32[]{:S(2)}, u32[]{:S(2)}) collective-permute-start(f32[80,128]{1,0:T(8,128)S(1)} %get-tuple-element.17.token.refs_0_.refs_1_), channel_id=1, source_target_pairs={{0,4},{1,5},{2,6},{3,7},{4,0},{5,1},{6,2},{7,3},{8,12},{9,13},{10,... | collective-permute-start | bytes 122888 | tf_op jit(solution)/shard_map/ppermute | solution.py:351
  7.3 0.0 copy-done.2
  7.3 0.0 copy-done
  7.3 0.0 copy-done.1
  7.3 3.0 %early.1 = (f32[5,5,256,128]{3,2,1,0:T(8,128)S(1)}, f32[5,272,128]{2,1,0:T(8,128)S(1)}, f32[5,64,128]{2,1,0:T(8,128)S(1)}) custom-call(f32[80,128]{1,0:T(8,128)S(1)} %get-tuple-element.17.token.refs_0_.refs_1_, f32[5,256,128]{2,1,0:T(8,128)S(1)} %copy-done.2, bf16[4,5,5,256,128]{4,3,2,1,0:T(8,128)(2,1)S(1)} %copy-done, f32[5,5,256,128]{3,2,1,0:T(8,128)S(1)} %copy-done.1), custom_call_target="tpu_custom_call" | custom-call | flops 20000000 | bytes 12582912 | tf_op jit(solution)/shard_map/early/pallas_call | solution.py:404
  10.3 0.0 collective-permute-done.refs_1_
  10.3 0.4 %collective-permute-done.1.refs_2_ = f32[80,128]{1,0:T(8,128)S(1)} collective-permute-done((f32[80,128]{1,0:T(8,128)S(1)}, f32[80,128]{1,0:T(8,128)S(1)}, u32[]{:S(2)}, u32[]{:S(2)}) %collective-permute-start.1) | collective-permute-done | bytes 40992 | tf_op jit(solution)/shard_map/ppermute | solution.py:351
  10.7 0.4 %collective-permute-done.2.refs_3_ = f32[80,128]{1,0:T(8,128)S(1)} collective-permute-done((f32[80,128]{1,0:T(8,128)S(1)}, f32[80,128]{1,0:T(8,128)S(1)}, u32[]{:S(2)}, u32[]{:S(2)}) %collective-permute-start.2) | collective-permute-done | bytes 40992 | tf_op jit(solution)/shard_map/ppermute | solution.py:351
  11.1 0.1 choose.1
  11.2 0.1 collective-permute-start.3
  11.3 1.6 %collective-permute-start.4 = (f32[80,128]{1,0:T(8,128)S(1)}, f32[80,128]{1,0:T(8,128)S(1)}, u32[]{:S(2)}, u32[]{:S(2)}) collective-permute-start(f32[80,128]{1,0:T(8,128)S(1)} %get-tuple-element.24), channel_id=1, source_target_pairs={{0,2},{1,3},{2,0},{3,1},{4,6},{5,7},{6,4},{7,5},{8,10},{9,11},{10,... | collective-permute-start | bytes 122888 | tf_op jit(solution)/shard_map/ppermute | solution.py:357
  12.8 0.3 %collective-permute-start.5 = (f32[80,128]{1,0:T(8,128)S(1)}, f32[80,128]{1,0:T(8,128)S(1)}, u32[]{:S(2)}, u32[]{:S(2)}) collective-permute-start(f32[80,128]{1,0:T(8,128)S(1)} %get-tuple-element.25), channel_id=1, source_target_pairs={{0,1},{1,0},{2,3},{3,2},{4,5},{5,4},{6,7},{7,6},{8,9},{9,8},{10,11... | collective-permute-start | bytes 122888 | tf_op jit(solution)/shard_map/ppermute | solution.py:357
  13.1 0.0 copy-start.3
  13.1 2.2 %late.1 = (f32[5,256,128]{2,1,0:T(8,128)}, f32[5,192,128]{2,1,0:T(8,128)S(1)}) custom-call(f32[5,256,128]{2,1,0:T(8,128)S(1)} %copy-done.2, bf16[4,5,5,256,128]{4,3,2,1,0:T(8,128)(2,1)S(1)} %copy-done, f32[5,5,256,128]{3,2,1,0:T(8,128)S(1)} %get-tuple-element.18.factors, f32[5,272,128]{2,1,0:T(8,128)S(1)} %get-tuple-element.19.first_sweep, ...), custom_call_target="tpu_custom_call" | custom-call | flops 8000000 | bytes 6291456 | tf_op jit(solution)/shard_map/late/pallas_call | solution.py:430
  15.3 0.0 collective-permute-done.3.refs_3_
  15.3 0.3 %collective-permute-done.4.refs_4_ = f32[80,128]{1,0:T(8,128)S(1)} collective-permute-done((f32[80,128]{1,0:T(8,128)S(1)}, f32[80,128]{1,0:T(8,128)S(1)}, u32[]{:S(2)}, u32[]{:S(2)}) %collective-permute-start.4) | collective-permute-done | bytes 40992 | tf_op jit(solution)/shard_map/ppermute | solution.py:357
  15.6 0.0 collective-permute-done.5.refs_5_
  15.6 0.0 copy-done.3
  15.6 0.9 %finish.1 = f32[5,256,128]{2,1,0:T(8,128)} custom-call(f32[5,256,128]{2,1,0:T(8,128)} %get-tuple-element.21.refs_0_, f32[80,128]{1,0:T(8,128)S(1)} %get-tuple-element.17.token.refs_0_.refs_1_, f32[80,128]{1,0:T(8,128)S(1)} %get-tuple-element.22.refs_2_, f32[80,128]{1,0:T(8,128)S(1)} %collective-permute-done.3.refs_3_, ...), custom_call_target="tpu_custom_call", output_to_operand_aliasing={{}: (0, {})} | custom-call | tf_op jit(solution)/shard_map/finish/pallas_call | solution.py:449
Async XLA Ops:
  0.0 7.3 %copy-start.2 = (f32[5,256,128]{2,1,0:T(8,128)S(1)}, f32[5,256,128]{2,1,0:T(8,128)}, u32[]{:S(2)}) copy-start(f32[5,256,128]{2,1,0:T(8,128)} %rhs.3) | copy-start | bytes 1966084
  0.0 7.3 %copy-start = (bf16[4,5,5,256,128]{4,3,2,1,0:T(8,128)(2,1)S(1)}, bf16[4,5,5,256,128]{4,3,2,1,0:T(8,128)(2,1)}, u32[]{:S(2)}) copy-start(bf16[4,5,5,256,128]{4,3,2,1,0:T(8,128)(2,1)} %off.3) | copy-start | bytes 19660804
  0.0 7.3 %copy-start.1 = (f32[5,5,256,128]{3,2,1,0:T(8,128)S(1)}, f32[5,5,256,128]{3,2,1,0:T(8,128)}, u32[]{:S(2)}) copy-start(f32[5,5,256,128]{3,2,1,0:T(8,128)} %diag.1) | copy-start | bytes 9830404
  1.6 8.7 %collective-permute-start = (f32[80,128]{1,0:T(8,128)S(1)}, f32[80,128]{1,0:T(8,128)S(1)}, u32[]{:S(2)}, u32[]{:S(2)}) collective-permute-start(f32[80,128]{1,0:T(8,128)S(1)} %get-tuple-element.17.token.refs_0_.refs_1_), channel_id=1, source_target_pairs={{0,8},{1,9},{2,10},{3,11},{4,12},{5,13},{6,14},{7,15},{8,4},{9,5},... | collective-permute-start | bytes 122888 | tf_op jit(solution)/shard_map/ppermute | solution.py:351
  5.7 5.0 %collective-permute-start.1 = (f32[80,128]{1,0:T(8,128)S(1)}, f32[80,128]{1,0:T(8,128)S(1)}, u32[]{:S(2)}, u32[]{:S(2)}) collective-permute-start(f32[80,128]{1,0:T(8,128)S(1)} %get-tuple-element.17.token.refs_0_.refs_1_), channel_id=1, source_target_pairs={{0,12},{1,13},{2,14},{3,15},{4,8},{5,9},{6,10},{7,11},{8,0},{9,1},... | collective-permute-start | bytes 122888 | tf_op jit(solution)/shard_map/ppermute | solution.py:351
  6.8 4.3 %collective-permute-start.2 = (f32[80,128]{1,0:T(8,128)S(1)}, f32[80,128]{1,0:T(8,128)S(1)}, u32[]{:S(2)}, u32[]{:S(2)}) collective-permute-start(f32[80,128]{1,0:T(8,128)S(1)} %get-tuple-element.17.token.refs_0_.refs_1_), channel_id=1, source_target_pairs={{0,4},{1,5},{2,6},{3,7},{4,0},{5,1},{6,2},{7,3},{8,12},{9,13},{10,... | collective-permute-start | bytes 122888 | tf_op jit(solution)/shard_map/ppermute | solution.py:351
  11.2 4.1 %collective-permute-start.3 = (f32[80,128]{1,0:T(8,128)S(1)}, f32[80,128]{1,0:T(8,128)S(1)}, u32[]{:S(2)}, u32[]{:S(2)}) collective-permute-start(f32[80,128]{1,0:T(8,128)S(1)} %get-tuple-element.23), channel_id=1, source_target_pairs={{0,3},{1,2},{2,1},{3,0},{4,7},{5,6},{6,5},{7,4},{8,11},{9,10},{10,... | collective-permute-start | bytes 122888 | tf_op jit(solution)/shard_map/ppermute | solution.py:357
  11.3 4.3 %collective-permute-start.4 = (f32[80,128]{1,0:T(8,128)S(1)}, f32[80,128]{1,0:T(8,128)S(1)}, u32[]{:S(2)}, u32[]{:S(2)}) collective-permute-start(f32[80,128]{1,0:T(8,128)S(1)} %get-tuple-element.24), channel_id=1, source_target_pairs={{0,2},{1,3},{2,0},{3,1},{4,6},{5,7},{6,4},{7,5},{8,10},{9,11},{10,... | collective-permute-start | bytes 122888 | tf_op jit(solution)/shard_map/ppermute | solution.py:357
  12.8 2.8 %collective-permute-start.5 = (f32[80,128]{1,0:T(8,128)S(1)}, f32[80,128]{1,0:T(8,128)S(1)}, u32[]{:S(2)}, u32[]{:S(2)}) collective-permute-start(f32[80,128]{1,0:T(8,128)S(1)} %get-tuple-element.25), channel_id=1, source_target_pairs={{0,1},{1,0},{2,3},{3,2},{4,5},{5,4},{6,7},{7,6},{8,9},{9,8},{10,11... | collective-permute-start | bytes 122888 | tf_op jit(solution)/shard_map/ppermute | solution.py:357
  13.1 2.5 %copy-start.3 = (s32[1,2,128]{2,1,0:T(2,128)S(1)}, s32[1,2,128]{2,1,0:T(2,128)}, u32[]{:S(2)}) copy-start(s32[1,2,128]{2,1,0:T(2,128)} %refs_6_.1) | copy-start | bytes 3076

commit v6 on v4

--- a/solution.py
+++ b/solution.py
@@ -13,9 +13,10 @@
 A_AT, M_AT, CODE_AT = 5, 10, 35
 PLANE = 4
 MIB = 2**20
-FACTOR_TILE, TILE = 32, 64
+FACTOR_TILE, TILE = 64, 64
 LINE_STEPS = ((2, 3, 1, 0), (3, 2, 0, 1), (1, 0, 3, 2))
-PLANE_STEPS = ((3, 2, 1, 0), (2, 3, 0, 1), (1, 0, 3, 2))
+LINE_FLIPS = (1, 1, 1)
+PLANE_STEPS = ((3, 2, 0, 1), (2, 3, 1, 0), (1, 0, 3, 2))
 
 
 def lu(entries):
@@ -260,7 +261,7 @@
         target = me - place + table(step, place)
         for slot in range(2):
             wanted = (2 * target + slot).astype(F32)
-            found = jnp.zeros((TOKEN, 128), F32)
+            found = jnp.full((TOKEN, 128), -1.0, F32)
             for token in tokens:
                 for side in range(2):
                     code = token[pl.ds(TOKEN * side + CODE_AT, 1)]
@@ -282,11 +283,9 @@
         half = slice(0, 8) if side == 0 else slice(8, 16)
         edge_row, next_row = (0, 1) if side == 0 else (7, 6)
         outer = outer_face(side)
-        source = own[pl.ds(at + CODE_AT, 1)].astype(jnp.int32) // 2
         found = arrived[0][pl.ds(at, TOKEN)]
-        for value, step in zip(arrived[1:], PLANE_STEPS):
-            sender = table([step.index(k) for k in range(PLANE)], me % PLANE)
-            here = lax.rem(source, PLANE) == sender
+        for value in arrived[1:]:
+            here = value[pl.ds(at + CODE_AT, 1)] == (2 * me + side).astype(F32)
             found = jnp.where(here, value[pl.ds(at, TOKEN)], found)
         columns = jnp.broadcast_to(order[0, side : side + 1], (8, 128))
         for first in (0, 8, 16, 24, TOKEN - 8):
@@ -345,8 +344,10 @@
     return pltpu.with_memory_space_constraint(value, pltpu.HBM)
 
 
-def along_line(value, step):
-    pairs = [(PLANE * k + j, PLANE * to + j) for k, to in enumerate(step) for j in range(PLANE)]
+def along_line(value, step, flip):
+    pairs = []
+    for k, to in enumerate(step):
+        pairs += [(PLANE * k + j, PLANE * to + (j ^ flip)) for j in range(PLANE)]
     return lax.ppermute(value, "blk", pairs)
 
 
@@ -390,10 +391,10 @@
 
     lines = count // PLANE
     if lines <= 8:
-        steps = [[k ^ by for k in range(lines)] for by in range(1, lines)]
+        steps = [([k ^ by for k in range(lines)], 0) for by in range(1, lines)]
         if lines == len(LINE_STEPS[0]):
-            steps = LINE_STEPS
-        tokens = [token] + [along_line(token, step) for step in steps]
+            steps = zip(LINE_STEPS, LINE_FLIPS)
+        tokens = [token] + [along_line(token, step, flip) for step, flip in steps]
     else:
         groups = [[PLANE * k + j for k in range(lines)] for j in range(PLANE)]
         gathered = lax.all_gather(token, "blk", axis_index_groups=groups)

time: 16.4 us -> 16.3 us (level)
    ppermute x3, waiting for transfers between devices: 0.01 us -> 0.41 us  [within_plane(): return lax.ppermute(value, 'blk', pairs)]
    ppermute x3, waiting for transfers between devices: 0.41 us -> 0.01 us  [along_line(): return lax.ppermute(value, 'blk', pairs)]
    ppermute x3, starting transfers between devices: 5.67 us -> 5.39 us  [along_line(): return lax.ppermute(value, 'blk', pairs)]
  transfers between devices with their start and end apart: 6 -> 6, of which waited for: 1 -> 1; matrix products, arithmetic and copies ran while one was open for 0% -> 0% of each run, Pallas kernels for 34% -> 35%
where the time goes in v6:
time: 16.3 us; the launch traced here: 16.2 us
  Pallas kernels  8.24 us (51%)
  starting transfers between devices  7.47 us (46%)
  waiting for transfers between devices  0.42 us (3%)
    ppermute x3, starting transfers between devices, along_line(): return lax.ppermute(value, 'blk', pairs)  5.39 us
    pallas_call x1, Pallas kernels, on_device(): pl.pallas_call(early_kernel, out_shape=(VMEM((5, 5, rows, 128), F32), VME...  3.36 us
    pallas_call x1, Pallas kernels, on_device(): pl.pallas_call(late_kernel, out_shape=(pltpu.HBM(right_side.shape, F32),...  2.29 us
    ppermute x3, starting transfers between devices, within_plane(): return lax.ppermute(value, 'blk', pairs)  2.08 us
    pallas_call x1, Pallas kernels, on_device(): pl.pallas_call(edge_kernel, out_shape=(VMEM((2 * TOKEN, 128), F32), VMEM(...  1.6 us
    pallas_call x1, Pallas kernels, on_device(): pl.pallas_call(finish_kernel, out_shape=pltpu.HBM(right_side.shape, F32),...  0.88 us
    ppermute x3, waiting for transfers between devices, within_plane(): return lax.ppermute(value, 'blk', pairs)  0.41 us
  transfers between devices with their start and end apart: 6, of which 1 were waited for; matrix products, arithmetic and copies ran while one was open for 0% of the time, Pallas kernels for 35%

profile of v6, /device:TPU:0, one launch (start us, length us, event | category | flops | bytes accessed | tf_op | source)
XLA Modules:
  0.0 16.2 jit_solution(10297071405603697793)
XLA Ops:
  0.0 0.0 copy-start.2
  0.0 0.0 copy-start
  0.0 0.0 copy-start.1
  0.0 1.6 %edges.1 = (f32[72,128]{1,0:T(8,128)S(1)}, f32[2,25,8,128]{3,2,1,0:T(8,128)S(1)}, bf16[2,4,5,5,16,128]{5,4,3,2,1,0:T(8,128)(2,1)S(1)}) custom-call(s32[16]{0:T(128)} %blocks_h.1, s32[1,2]{1,0:T(1,128)} %pairs_h.1, f32[5,256,128]{2,1,0:T(8,128)} %rhs.3, bf16[4,5,5,256,128]{4,3,2,1,0:T(8,128)(2,1)} %off.3, f32[5,5,256,128]{3,2,1,0:T(8,128)} %diag.1), custom_call_target="tpu_custom_call" | custom-call | tf_op jit(solution)/shard_map/edges/pallas_call | solution.py:365
  1.6 3.5 %collective-permute-start = (f32[72,128]{1,0:T(8,128)S(1)}, f32[72,128]{1,0:T(8,128)S(1)}, u32[]{:S(2)}, u32[]{:S(2)}) collective-permute-start(f32[72,128]{1,0:T(8,128)S(1)} %get-tuple-element.17.token.refs_0_.refs_1_), channel_id=1, source_target_pairs={{0,9},{1,8},{2,11},{3,10},{4,13},{5,12},{6,15},{7,14},{8,5},{9,4},... | collective-permute-start | bytes 110600 | tf_op jit(solution)/shard_map/ppermute | solution.py:351
  5.1 1.1 %collective-permute-start.1 = (f32[72,128]{1,0:T(8,128)S(1)}, f32[72,128]{1,0:T(8,128)S(1)}, u32[]{:S(2)}, u32[]{:S(2)}) collective-permute-start(f32[72,128]{1,0:T(8,128)S(1)} %get-tuple-element.17.token.refs_0_.refs_1_), channel_id=1, source_target_pairs={{0,13},{1,12},{2,15},{3,14},{4,9},{5,8},{6,11},{7,10},{8,1},{9,0},... | collective-permute-start | bytes 110600 | tf_op jit(solution)/shard_map/ppermute | solution.py:351
  6.2 0.8 %collective-permute-start.2 = (f32[72,128]{1,0:T(8,128)S(1)}, f32[72,128]{1,0:T(8,128)S(1)}, u32[]{:S(2)}, u32[]{:S(2)}) collective-permute-start(f32[72,128]{1,0:T(8,128)S(1)} %get-tuple-element.17.token.refs_0_.refs_1_), channel_id=1, source_target_pairs={{0,5},{1,4},{2,7},{3,6},{4,1},{5,0},{6,3},{7,2},{8,13},{9,12},{10,... | collective-permute-start | bytes 110600 | tf_op jit(solution)/shard_map/ppermute | solution.py:351
  7.0 0.0 copy-done.2
  7.0 0.0 copy-done
  7.0 0.0 copy-done.1
  7.0 3.4 %early.1 = (f32[5,5,256,128]{3,2,1,0:T(8,128)S(1)}, f32[5,272,128]{2,1,0:T(8,128)S(1)}, f32[5,64,128]{2,1,0:T(8,128)S(1)}) custom-call(f32[72,128]{1,0:T(8,128)S(1)} %get-tuple-element.17.token.refs_0_.refs_1_, f32[5,256,128]{2,1,0:T(8,128)S(1)} %copy-done.2, bf16[4,5,5,256,128]{4,3,2,1,0:T(8,128)(2,1)S(1)} %copy-done, f32[5,5,256,128]{3,2,1,0:T(8,128)S(1)} %copy-done.1), custom_call_target="tpu_custom_call" | custom-call | flops 20000000 | bytes 12582912 | tf_op jit(solution)/shard_map/early/pallas_call | solution.py:404
  10.4 0.0 collective-permute-done.refs_1_
  10.4 0.0 collective-permute-done.1.refs_2_
  10.4 0.0 collective-permute-done.2.refs_3_
  10.4 0.1 choose.1
  10.5 1.4 %collective-permute-start.3 = (f32[72,128]{1,0:T(8,128)S(1)}, f32[72,128]{1,0:T(8,128)S(1)}, u32[]{:S(2)}, u32[]{:S(2)}) collective-permute-start(f32[72,128]{1,0:T(8,128)S(1)} %get-tuple-element.23), channel_id=1, source_target_pairs={{0,3},{1,2},{2,0},{3,1},{4,7},{5,6},{6,4},{7,5},{8,11},{9,10},{10,... | collective-permute-start | bytes 110600 | tf_op jit(solution)/shard_map/ppermute | solution.py:357
  11.9 0.7 %collective-permute-start.4 = (f32[72,128]{1,0:T(8,128)S(1)}, f32[72,128]{1,0:T(8,128)S(1)}, u32[]{:S(2)}, u32[]{:S(2)}) collective-permute-start(f32[72,128]{1,0:T(8,128)S(1)} %get-tuple-element.24), channel_id=1, source_target_pairs={{0,2},{1,3},{2,1},{3,0},{4,6},{5,7},{6,5},{7,4},{8,10},{9,11},{10,... | collective-permute-start | bytes 110600 | tf_op jit(solution)/shard_map/ppermute | solution.py:357
  12.6 0.0 collective-permute-start.5
  12.6 0.0 copy-start.3
  12.6 2.3 %late.1 = (f32[5,256,128]{2,1,0:T(8,128)}, f32[5,192,128]{2,1,0:T(8,128)S(1)}) custom-call(f32[5,256,128]{2,1,0:T(8,128)S(1)} %copy-done.2, bf16[4,5,5,256,128]{4,3,2,1,0:T(8,128)(2,1)S(1)} %copy-done, f32[5,5,256,128]{3,2,1,0:T(8,128)S(1)} %get-tuple-element.18.factors, f32[5,272,128]{2,1,0:T(8,128)S(1)} %get-tuple-element.19.first_sweep, ...), custom_call_target="tpu_custom_call" | custom-call | flops 8000000 | bytes 6291456 | tf_op jit(solution)/shard_map/late/pallas_call | solution.py:430
  14.9 0.0 collective-permute-done.3.refs_3_
  14.9 0.4 %collective-permute-done.4.refs_4_ = f32[72,128]{1,0:T(8,128)S(1)} collective-permute-done((f32[72,128]{1,0:T(8,128)S(1)}, f32[72,128]{1,0:T(8,128)S(1)}, u32[]{:S(2)}, u32[]{:S(2)}) %collective-permute-start.4) | collective-permute-done | bytes 36896 | tf_op jit(solution)/shard_map/ppermute | solution.py:357
  15.3 0.0 collective-permute-done.5.refs_5_
  15.3 0.0 copy-done.3
  15.3 0.9 %finish.1 = f32[5,256,128]{2,1,0:T(8,128)} custom-call(f32[5,256,128]{2,1,0:T(8,128)} %get-tuple-element.21.refs_0_, f32[72,128]{1,0:T(8,128)S(1)} %get-tuple-element.17.token.refs_0_.refs_1_, f32[72,128]{1,0:T(8,128)S(1)} %get-tuple-element.22.refs_2_, f32[72,128]{1,0:T(8,128)S(1)} %collective-permute-done.3.refs_3_, ...), custom_call_target="tpu_custom_call", output_to_operand_aliasing={{}: (0, {})} | custom-call | tf_op jit(solution)/shard_map/finish/pallas_call | solution.py:449
Async XLA Ops:
  0.0 7.0 %copy-start.2 = (f32[5,256,128]{2,1,0:T(8,128)S(1)}, f32[5,256,128]{2,1,0:T(8,128)}, u32[]{:S(2)}) copy-start(f32[5,256,128]{2,1,0:T(8,128)} %rhs.3) | copy-start | bytes 1966084
  0.0 7.0 %copy-start = (bf16[4,5,5,256,128]{4,3,2,1,0:T(8,128)(2,1)S(1)}, bf16[4,5,5,256,128]{4,3,2,1,0:T(8,128)(2,1)}, u32[]{:S(2)}) copy-start(bf16[4,5,5,256,128]{4,3,2,1,0:T(8,128)(2,1)} %off.3) | copy-start | bytes 19660804
  0.0 7.0 %copy-start.1 = (f32[5,5,256,128]{3,2,1,0:T(8,128)S(1)}, f32[5,5,256,128]{3,2,1,0:T(8,128)}, u32[]{:S(2)}) copy-start(f32[5,5,256,128]{3,2,1,0:T(8,128)} %diag.1) | copy-start | bytes 9830404
  1.6 8.8 %collective-permute-start = (f32[72,128]{1,0:T(8,128)S(1)}, f32[72,128]{1,0:T(8,128)S(1)}, u32[]{:S(2)}, u32[]{:S(2)}) collective-permute-start(f32[72,128]{1,0:T(8,128)S(1)} %get-tuple-element.17.token.refs_0_.refs_1_), channel_id=1, source_target_pairs={{0,9},{1,8},{2,11},{3,10},{4,13},{5,12},{6,15},{7,14},{8,5},{9,4},... | collective-permute-start | bytes 110600 | tf_op jit(solution)/shard_map/ppermute | solution.py:351
  5.1 5.2 %collective-permute-start.1 = (f32[72,128]{1,0:T(8,128)S(1)}, f32[72,128]{1,0:T(8,128)S(1)}, u32[]{:S(2)}, u32[]{:S(2)}) collective-permute-start(f32[72,128]{1,0:T(8,128)S(1)} %get-tuple-element.17.token.refs_0_.refs_1_), channel_id=1, source_target_pairs={{0,13},{1,12},{2,15},{3,14},{4,9},{5,8},{6,11},{7,10},{8,1},{9,0},... | collective-permute-start | bytes 110600 | tf_op jit(solution)/shard_map/ppermute | solution.py:351
  6.2 4.2 %collective-permute-start.2 = (f32[72,128]{1,0:T(8,128)S(1)}, f32[72,128]{1,0:T(8,128)S(1)}, u32[]{:S(2)}, u32[]{:S(2)}) collective-permute-start(f32[72,128]{1,0:T(8,128)S(1)} %get-tuple-element.17.token.refs_0_.refs_1_), channel_id=1, source_target_pairs={{0,5},{1,4},{2,7},{3,6},{4,1},{5,0},{6,3},{7,2},{8,13},{9,12},{10,... | collective-permute-start | bytes 110600 | tf_op jit(solution)/shard_map/ppermute | solution.py:351
  10.5 4.4 %collective-permute-start.3 = (f32[72,128]{1,0:T(8,128)S(1)}, f32[72,128]{1,0:T(8,128)S(1)}, u32[]{:S(2)}, u32[]{:S(2)}) collective-permute-start(f32[72,128]{1,0:T(8,128)S(1)} %get-tuple-element.23), channel_id=1, source_target_pairs={{0,3},{1,2},{2,0},{3,1},{4,7},{5,6},{6,4},{7,5},{8,11},{9,10},{10,... | collective-permute-start | bytes 110600 | tf_op jit(solution)/shard_map/ppermute | solution.py:357
  11.9 3.4 %collective-permute-start.4 = (f32[72,128]{1,0:T(8,128)S(1)}, f32[72,128]{1,0:T(8,128)S(1)}, u32[]{:S(2)}, u32[]{:S(2)}) collective-permute-start(f32[72,128]{1,0:T(8,128)S(1)} %get-tuple-element.24), channel_id=1, source_target_pairs={{0,2},{1,3},{2,1},{3,0},{4,6},{5,7},{6,5},{7,4},{8,10},{9,11},{10,... | collective-permute-start | bytes 110600 | tf_op jit(solution)/shard_map/ppermute | solution.py:357
  12.6 2.7 %collective-permute-start.5 = (f32[72,128]{1,0:T(8,128)S(1)}, f32[72,128]{1,0:T(8,128)S(1)}, u32[]{:S(2)}, u32[]{:S(2)}) collective-permute-start(f32[72,128]{1,0:T(8,128)S(1)} %get-tuple-element.25), channel_id=1, source_target_pairs={{0,1},{1,0},{2,3},{3,2},{4,5},{5,4},{6,7},{7,6},{8,9},{9,8},{10,11... | collective-permute-start | bytes 110600 | tf_op jit(solution)/shard_map/ppermute | solution.py:357
  12.6 2.7 %copy-start.3 = (s32[1,2,128]{2,1,0:T(2,128)S(1)}, s32[1,2,128]{2,1,0:T(2,128)}, u32[]{:S(2)}) copy-start(s32[1,2,128]{2,1,0:T(2,128)} %refs_6_.1) | copy-start | bytes 3076

commit v7 on v6

--- a/solution.py
+++ b/solution.py
@@ -13,7 +13,7 @@
 A_AT, M_AT, CODE_AT = 5, 10, 35
 PLANE = 4
 MIB = 2**20
-FACTOR_TILE, TILE = 64, 64
+FACTOR_TILE, TILE = 128, 64
 LINE_STEPS = ((2, 3, 1, 0), (3, 2, 0, 1), (1, 0, 3, 2))
 LINE_FLIPS = (1, 1, 1)
 PLANE_STEPS = ((3, 2, 0, 1), (2, 3, 1, 0), (1, 0, 3, 2))

time: 16.3 us -> 16.3 us (level)
  no operation moved by 1% of the time
where the time goes in v7:
time: 16.3 us; the launch traced here: 16.2 us
  Pallas kernels  8.26 us (51%)
  starting transfers between devices  7.47 us (46%)
  waiting for transfers between devices  0.39 us (2%)
    ppermute x3, starting transfers between devices, along_line(): return lax.ppermute(value, 'blk', pairs)  5.39 us
    pallas_call x1, Pallas kernels, on_device(): pl.pallas_call(early_kernel, out_shape=(VMEM((5, 5, rows, 128), F32), VME...  3.38 us
    pallas_call x1, Pallas kernels, on_device(): pl.pallas_call(late_kernel, out_shape=(pltpu.HBM(right_side.shape, F32),...  2.29 us
    ppermute x3, starting transfers between devices, within_plane(): return lax.ppermute(value, 'blk', pairs)  2.08 us
    pallas_call x1, Pallas kernels, on_device(): pl.pallas_call(edge_kernel, out_shape=(VMEM((2 * TOKEN, 128), F32), VMEM(...  1.6 us
    pallas_call x1, Pallas kernels, on_device(): pl.pallas_call(finish_kernel, out_shape=pltpu.HBM(right_side.shape, F32),...  0.88 us
    ppermute x3, waiting for transfers between devices, within_plane(): return lax.ppermute(value, 'blk', pairs)  0.39 us
  transfers between devices with their start and end apart: 6, of which 1 were waited for; matrix products, arithmetic and copies ran while one was open for 0% of the time, Pallas kernels for 35%

profile of v7, /device:TPU:0, one launch (start us, length us, event | category | flops | bytes accessed | tf_op | source)
XLA Modules:
  0.0 16.2 jit_solution(7207722778040137207)
XLA Ops:
  0.0 0.0 copy-start.2
  0.0 0.0 copy-start
  0.0 0.0 copy-start.1
  0.0 1.6 %edges.1 = (f32[72,128]{1,0:T(8,128)S(1)}, f32[2,25,8,128]{3,2,1,0:T(8,128)S(1)}, bf16[2,4,5,5,16,128]{5,4,3,2,1,0:T(8,128)(2,1)S(1)}) custom-call(s32[16]{0:T(128)} %blocks_h.1, s32[1,2]{1,0:T(1,128)} %pairs_h.1, f32[5,256,128]{2,1,0:T(8,128)} %rhs.3, bf16[4,5,5,256,128]{4,3,2,1,0:T(8,128)(2,1)} %off.3, f32[5,5,256,128]{3,2,1,0:T(8,128)} %diag.1), custom_call_target="tpu_custom_call" | custom-call | tf_op jit(solution)/shard_map/edges/pallas_call | solution.py:365
  1.6 3.5 %collective-permute-start = (f32[72,128]{1,0:T(8,128)S(1)}, f32[72,128]{1,0:T(8,128)S(1)}, u32[]{:S(2)}, u32[]{:S(2)}) collective-permute-start(f32[72,128]{1,0:T(8,128)S(1)} %get-tuple-element.17.token.refs_0_.refs_1_), channel_id=1, source_target_pairs={{0,9},{1,8},{2,11},{3,10},{4,13},{5,12},{6,15},{7,14},{8,5},{9,4},... | collective-permute-start | bytes 110600 | tf_op jit(solution)/shard_map/ppermute | solution.py:351
  5.1 1.1 %collective-permute-start.1 = (f32[72,128]{1,0:T(8,128)S(1)}, f32[72,128]{1,0:T(8,128)S(1)}, u32[]{:S(2)}, u32[]{:S(2)}) collective-permute-start(f32[72,128]{1,0:T(8,128)S(1)} %get-tuple-element.17.token.refs_0_.refs_1_), channel_id=1, source_target_pairs={{0,13},{1,12},{2,15},{3,14},{4,9},{5,8},{6,11},{7,10},{8,1},{9,0},... | collective-permute-start | bytes 110600 | tf_op jit(solution)/shard_map/ppermute | solution.py:351
  6.2 0.8 %collective-permute-start.2 = (f32[72,128]{1,0:T(8,128)S(1)}, f32[72,128]{1,0:T(8,128)S(1)}, u32[]{:S(2)}, u32[]{:S(2)}) collective-permute-start(f32[72,128]{1,0:T(8,128)S(1)} %get-tuple-element.17.token.refs_0_.refs_1_), channel_id=1, source_target_pairs={{0,5},{1,4},{2,7},{3,6},{4,1},{5,0},{6,3},{7,2},{8,13},{9,12},{10,... | collective-permute-start | bytes 110600 | tf_op jit(solution)/shard_map/ppermute | solution.py:351
  7.0 0.0 copy-done.2
  7.0 0.0 copy-done
  7.0 0.0 copy-done.1
  7.0 3.4 %early.1 = (f32[5,5,256,128]{3,2,1,0:T(8,128)S(1)}, f32[5,272,128]{2,1,0:T(8,128)S(1)}, f32[5,64,128]{2,1,0:T(8,128)S(1)}) custom-call(f32[72,128]{1,0:T(8,128)S(1)} %get-tuple-element.17.token.refs_0_.refs_1_, f32[5,256,128]{2,1,0:T(8,128)S(1)} %copy-done.2, bf16[4,5,5,256,128]{4,3,2,1,0:T(8,128)(2,1)S(1)} %copy-done, f32[5,5,256,128]{3,2,1,0:T(8,128)S(1)} %copy-done.1), custom_call_target="tpu_custom_call" | custom-call | flops 20000000 | bytes 12582912 | tf_op jit(solution)/shard_map/early/pallas_call | solution.py:404
  10.4 0.0 collective-permute-done.refs_1_
  10.4 0.0 collective-permute-done.1.refs_2_
  10.4 0.0 collective-permute-done.2.refs_3_
  10.4 0.1 choose.1
  10.5 1.4 %collective-permute-start.3 = (f32[72,128]{1,0:T(8,128)S(1)}, f32[72,128]{1,0:T(8,128)S(1)}, u32[]{:S(2)}, u32[]{:S(2)}) collective-permute-start(f32[72,128]{1,0:T(8,128)S(1)} %get-tuple-element.23), channel_id=1, source_target_pairs={{0,3},{1,2},{2,0},{3,1},{4,7},{5,6},{6,4},{7,5},{8,11},{9,10},{10,... | collective-permute-start | bytes 110600 | tf_op jit(solution)/shard_map/ppermute | solution.py:357
  11.9 0.7 %collective-permute-start.4 = (f32[72,128]{1,0:T(8,128)S(1)}, f32[72,128]{1,0:T(8,128)S(1)}, u32[]{:S(2)}, u32[]{:S(2)}) collective-permute-start(f32[72,128]{1,0:T(8,128)S(1)} %get-tuple-element.24), channel_id=1, source_target_pairs={{0,2},{1,3},{2,1},{3,0},{4,6},{5,7},{6,5},{7,4},{8,10},{9,11},{10,... | collective-permute-start | bytes 110600 | tf_op jit(solution)/shard_map/ppermute | solution.py:357
  12.6 0.0 collective-permute-start.5
  12.6 0.0 copy-start.3
  12.6 2.3 %late.1 = (f32[5,256,128]{2,1,0:T(8,128)}, f32[5,192,128]{2,1,0:T(8,128)S(1)}) custom-call(f32[5,256,128]{2,1,0:T(8,128)S(1)} %copy-done.2, bf16[4,5,5,256,128]{4,3,2,1,0:T(8,128)(2,1)S(1)} %copy-done, f32[5,5,256,128]{3,2,1,0:T(8,128)S(1)} %get-tuple-element.18.factors, f32[5,272,128]{2,1,0:T(8,128)S(1)} %get-tuple-element.19.first_sweep, ...), custom_call_target="tpu_custom_call" | custom-call | flops 8000000 | bytes 6291456 | tf_op jit(solution)/shard_map/late/pallas_call | solution.py:430
  14.9 0.0 collective-permute-done.3.refs_3_
  14.9 0.4 %collective-permute-done.4.refs_4_ = f32[72,128]{1,0:T(8,128)S(1)} collective-permute-done((f32[72,128]{1,0:T(8,128)S(1)}, f32[72,128]{1,0:T(8,128)S(1)}, u32[]{:S(2)}, u32[]{:S(2)}) %collective-permute-start.4) | collective-permute-done | bytes 36896 | tf_op jit(solution)/shard_map/ppermute | solution.py:357
  15.3 0.0 collective-permute-done.5.refs_5_
  15.3 0.0 copy-done.3
  15.3 0.9 %finish.1 = f32[5,256,128]{2,1,0:T(8,128)} custom-call(f32[5,256,128]{2,1,0:T(8,128)} %get-tuple-element.21.refs_0_, f32[72,128]{1,0:T(8,128)S(1)} %get-tuple-element.17.token.refs_0_.refs_1_, f32[72,128]{1,0:T(8,128)S(1)} %get-tuple-element.22.refs_2_, f32[72,128]{1,0:T(8,128)S(1)} %collective-permute-done.3.refs_3_, ...), custom_call_target="tpu_custom_call", output_to_operand_aliasing={{}: (0, {})} | custom-call | tf_op jit(solution)/shard_map/finish/pallas_call | solution.py:449
Async XLA Ops:
  0.0 7.0 %copy-start.2 = (f32[5,256,128]{2,1,0:T(8,128)S(1)}, f32[5,256,128]{2,1,0:T(8,128)}, u32[]{:S(2)}) copy-start(f32[5,256,128]{2,1,0:T(8,128)} %rhs.3) | copy-start | bytes 1966084
  0.0 7.0 %copy-start = (bf16[4,5,5,256,128]{4,3,2,1,0:T(8,128)(2,1)S(1)}, bf16[4,5,5,256,128]{4,3,2,1,0:T(8,128)(2,1)}, u32[]{:S(2)}) copy-start(bf16[4,5,5,256,128]{4,3,2,1,0:T(8,128)(2,1)} %off.3) | copy-start | bytes 19660804
  0.0 7.0 %copy-start.1 = (f32[5,5,256,128]{3,2,1,0:T(8,128)S(1)}, f32[5,5,256,128]{3,2,1,0:T(8,128)}, u32[]{:S(2)}) copy-start(f32[5,5,256,128]{3,2,1,0:T(8,128)} %diag.1) | copy-start | bytes 9830404
  1.6 8.8 %collective-permute-start = (f32[72,128]{1,0:T(8,128)S(1)}, f32[72,128]{1,0:T(8,128)S(1)}, u32[]{:S(2)}, u32[]{:S(2)}) collective-permute-start(f32[72,128]{1,0:T(8,128)S(1)} %get-tuple-element.17.token.refs_0_.refs_1_), channel_id=1, source_target_pairs={{0,9},{1,8},{2,11},{3,10},{4,13},{5,12},{6,15},{7,14},{8,5},{9,4},... | collective-permute-start | bytes 110600 | tf_op jit(solution)/shard_map/ppermute | solution.py:351
  5.1 5.3 %collective-permute-start.1 = (f32[72,128]{1,0:T(8,128)S(1)}, f32[72,128]{1,0:T(8,128)S(1)}, u32[]{:S(2)}, u32[]{:S(2)}) collective-permute-start(f32[72,128]{1,0:T(8,128)S(1)} %get-tuple-element.17.token.refs_0_.refs_1_), channel_id=1, source_target_pairs={{0,13},{1,12},{2,15},{3,14},{4,9},{5,8},{6,11},{7,10},{8,1},{9,0},... | collective-permute-start | bytes 110600 | tf_op jit(solution)/shard_map/ppermute | solution.py:351
  6.2 4.2 %collective-permute-start.2 = (f32[72,128]{1,0:T(8,128)S(1)}, f32[72,128]{1,0:T(8,128)S(1)}, u32[]{:S(2)}, u32[]{:S(2)}) collective-permute-start(f32[72,128]{1,0:T(8,128)S(1)} %get-tuple-element.17.token.refs_0_.refs_1_), channel_id=1, source_target_pairs={{0,5},{1,4},{2,7},{3,6},{4,1},{5,0},{6,3},{7,2},{8,13},{9,12},{10,... | collective-permute-start | bytes 110600 | tf_op jit(solution)/shard_map/ppermute | solution.py:351
  10.5 4.4 %collective-permute-start.3 = (f32[72,128]{1,0:T(8,128)S(1)}, f32[72,128]{1,0:T(8,128)S(1)}, u32[]{:S(2)}, u32[]{:S(2)}) collective-permute-start(f32[72,128]{1,0:T(8,128)S(1)} %get-tuple-element.23), channel_id=1, source_target_pairs={{0,3},{1,2},{2,0},{3,1},{4,7},{5,6},{6,4},{7,5},{8,11},{9,10},{10,... | collective-permute-start | bytes 110600 | tf_op jit(solution)/shard_map/ppermute | solution.py:357
  11.9 3.4 %collective-permute-start.4 = (f32[72,128]{1,0:T(8,128)S(1)}, f32[72,128]{1,0:T(8,128)S(1)}, u32[]{:S(2)}, u32[]{:S(2)}) collective-permute-start(f32[72,128]{1,0:T(8,128)S(1)} %get-tuple-element.24), channel_id=1, source_target_pairs={{0,2},{1,3},{2,1},{3,0},{4,6},{5,7},{6,5},{7,4},{8,10},{9,11},{10,... | collective-permute-start | bytes 110600 | tf_op jit(solution)/shard_map/ppermute | solution.py:357
  12.6 2.7 %collective-permute-start.5 = (f32[72,128]{1,0:T(8,128)S(1)}, f32[72,128]{1,0:T(8,128)S(1)}, u32[]{:S(2)}, u32[]{:S(2)}) collective-permute-start(f32[72,128]{1,0:T(8,128)S(1)} %get-tuple-element.25), channel_id=1, source_target_pairs={{0,1},{1,0},{2,3},{3,2},{4,5},{5,4},{6,7},{7,6},{8,9},{9,8},{10,11... | collective-permute-start | bytes 110600 | tf_op jit(solution)/shard_map/ppermute | solution.py:357
  12.6 2.7 %copy-start.3 = (s32[1,2,128]{2,1,0:T(2,128)S(1)}, s32[1,2,128]{2,1,0:T(2,128)}, u32[]{:S(2)}) copy-start(s32[1,2,128]{2,1,0:T(2,128)} %refs_6_.1) | copy-start | bytes 3076
